TPU v7x, 128 devices: a whole 4x4x4 slice. The times are simulated.
128 devices in a mesh: row: 16 (over z, y_hi, core), col: 8 (over y_lo, x).
Axes of the slice: x: 4, y: 4 (y_hi: 2, y_lo: 2; y = y_hi * 2 + y_lo), z: 4, core: 2. Of those that a mesh axis runs over, the one named last changes fastest.
Arguments:
- features: bfloat16 [131072, 64], P(('col', 'row')), may hold values from -6 to 6
- weight: bfloat16 [64, 256], replicated, may hold values from -0.75 to 0.75
- cotangent: bfloat16 [131072, 256], P(('row', 'col')), may hold values from -6 to 6
- tile_values: bfloat16 [16, 8, 384, 128, 128], P('row', 'col'), may hold values from -0.25 to 0.25
- tile_rows: int32 [16, 8, 384], P('row', 'col'), may hold values from 0 to 63
- tile_cols: int32 [16, 8, 384], P('row', 'col'), may hold values from 0 to 127
- tile_counts: int32 [16, 8], P('row', 'col'), may hold values from 1 to 384, as said below
Outputs:
- activations: bfloat16 [131072, 256], P(('row', 'col'))
- feature_grad: bfloat16 [131072, 64], P(('col', 'row'))
- weight_grad: float32 [64, 256], replicated
Inputs may be any that keep to these rules, and one draw needn't show every extreme that they name: `tile_counts`: each grid block's number of live tile slots; some grid block uses all 384 slots.
All inputs are finite; a program needn't handle non-finite values.
Results may differ from a plain program's by a relative error of at most 0.006.
Values may be sent and summed in bfloat16 or wider, within the bound.
No kernel may reach another device: no remote copies, remote signals or barrier semaphores. Data moves between devices by JAX's collectives and lax.ppermute only.
A program may use at most 128 MiB of HBM per device.

v0:
```python
import jax
import jax.numpy as jnp
from jax import lax
from jax.sharding import PartitionSpec as P


def tile_pass(values, targets, picks, live, source, out_rows, transpose, first_tile):
    side = values.shape[1]
    width = source.shape[1]
    block_size = 64
    tiled = source.reshape(-1, side, width)
    out_tiles = out_rows // side
    rounds = (live + block_size - 1) // block_size

    def advance(number, totals):
        first = number * block_size
        block_values = lax.dynamic_slice_in_dim(values, first, block_size, 0)
        target = lax.dynamic_slice_in_dim(targets, first, block_size, 0) - first_tile
        pick = lax.dynamic_slice_in_dim(picks, first, block_size, 0)
        inside = first + jnp.arange(block_size, dtype=jnp.int32) < live
        inside = inside & (target >= 0) & (target < out_tiles)
        target = jnp.clip(target, 0, out_tiles - 1)
        picked = tiled[pick]
        if transpose:
            product = jnp.einsum(
                "tji,tjf->tif", block_values, picked, preferred_element_type=jnp.float32
            )
        else:
            product = jnp.einsum(
                "tij,tjf->tif", block_values, picked, preferred_element_type=jnp.float32
            )
        product = jnp.where(inside[:, None, None], product, 0.0)
        return totals.at[target].add(product)

    start = jnp.zeros((out_tiles, side, width), jnp.float32)
    totals = lax.fori_loop(0, rounds, advance, start)
    return totals.reshape(out_rows, width)


def backward_local(pre, cotangent):
    sigma = jax.nn.sigmoid(pre)
    pre_grad = (cotangent.astype(jnp.float32) * sigma * (1.0 + pre * (1.0 - sigma))).astype(
        jnp.bfloat16
    )
    return pre_grad


def on_device(features, weight, cotangent, tile_values, tile_rows, tile_cols, tile_counts):
    own_rows = features.shape[0]
    values = tile_values[0, 0]
    rows = tile_rows[0, 0]
    cols = tile_cols[0, 0]
    live = tile_counts[0, 0]
    block_rows = own_rows * lax.axis_size("col")
    sources = lax.all_gather(features, "row", axis=0, tiled=True)
    partial_value = tile_pass(values, rows, cols, live, sources, block_rows, False, 0)
    shares = lax.psum_scatter(partial_value, "col", scatter_dimension=0, tiled=True)
    shares_low = shares.astype(jnp.bfloat16)
    pre = jnp.dot(shares_low, weight, preferred_element_type=jnp.float32)
    activations = jax.nn.silu(pre).astype(jnp.bfloat16)
    pre_grad = backward_local(pre, cotangent)
    own_grad = jnp.dot(pre_grad, weight.T, preferred_element_type=jnp.float32).astype(jnp.bfloat16)
    weight_part = jnp.dot(shares_low.T, pre_grad, preferred_element_type=jnp.float32)
    grad_block = lax.all_gather(own_grad, "col", axis=0, tiled=True)
    source_rows = own_rows * lax.axis_size("row")
    grad_partial = tile_pass(values, cols, rows, live, grad_block, source_rows, True, 0)
    feature_grad = lax.psum_scatter(grad_partial, "row", scatter_dimension=0, tiled=True).astype(
        jnp.bfloat16
    )
    weight_grad = lax.psum(weight_part, ("row", "col"))
    return (activations, feature_grad, weight_grad)


def solution(mesh):
    in_specs = (
        P(("col", "row"), None),
        P(),
        P(("row", "col"), None),
        P("row", "col", None, None, None),
        P("row", "col", None),
        P("row", "col", None),
        P("row", "col"),
    )
    out_specs = (P(("row", "col"), None), P(("col", "row"), None), P())
    return jax.shard_map(
        on_device, mesh=mesh, in_specs=in_specs, out_specs=out_specs, check_vma=False
    )
```

profile of v0, /device:TPU:0, one launch (start us, length us, event | category | flops | bytes accessed | tf_op | source)
XLA Modules:
  0.0 595.8 jit_solution(8431483876171485664)
XLA Ops:
  7.2 0.7 all-gather.3.cloned.1.call-update
  8.6 0.7 reduce
  9.3 0.7 reduce.1
  10.0 50.6 %all-gather.3.cloned.1.call-done = bf16[16384,64]{0,1:T(8,128)(2,1)} async-done(((bf16[1024,64]{0,1:T(8,128)(2,1)}), bf16[16384,64]{0,1:T(8,128)(2,1)}) %all-gather.3.cloned.1.call-update) | async-done | bytes 2097168 | tf_op jit(solution)/shard_map/all_gather | solution.py:55
  60.6 4.8 copy.17
  65.4 1.6 broadcast_in_dim.40
  66.9 18.0 %while.20 = (s32[]{:T(128)}, f32[64,128,64]{1,2,0:T(8,128)}, s32[]{:T(128)}, s32[384]{0:T(512)S(1)}, s32[]{:T(128)}, /*index=5*/bf16[384,128,128]{2,1,0:T(8,128)...) while((s32[]{:T(128)}, f32[64,128,64]{1,2,0:T(8,128)}, ...), condition=%wide.region_2.3_spmd, body=%wide.region_0.2_spmd.sunk | while | flops 135268160 | bytes 14686519 | solution.py:36
  66.9 0.7 compare_and_fusion.4
  67.7 0.1 compare_select_fusion.6
  67.7 4.4 gather_fusion
  72.1 3.7 fusion.32
  75.8 9.1 %scatter_fusion = f32[64,128,64]{1,2,0:T(8,128)} fusion(f32[64,128,64]{1,2,0:T(8,128)} %get-tuple-element.266, s32[64]{0:T(128)S(1)} %get-tuple-element.241, f32[64,128,64]{1,2,0:T(8,128)S(1)} %fusion.32), kind=kCustom, calls=%fused_computation.2.clone.1 | custom fusion | flops 524288 | bytes 6291712 | tf_op jit(solution)/shard_map/while/body/scatter-add | solution.py:33
  85.0 3.1 copy_bitcast_fusion.1
  88.1 130.7 %reduce-scatter.3.cloned.1.call-done = f32[1024,64]{0,1:T(8,128)} async-done(((f32[8192,64]{0,1:T(8,128)}), f32[1024,64]{0,1:T(8,128)}) %reduce-scatter.3.cloned.1.call-update) | async-done | bytes 262160 | tf_op jit(solution)/shard_map/reduce_scatter | solution.py:57
  218.8 2.4 multiply_convert_fusion
  221.2 0.9 convolution_convert_fusion
  222.2 37.7 %all-gather.5.cloned.1.call-done = bf16[8192,64]{0,1:T(8,128)(2,1)} async-done(((bf16[1024,64]{0,1:T(8,128)(2,1)}), bf16[8192,64]{0,1:T(8,128)(2,1)}) %all-gather.5.cloned.1.call-update) | async-done | bytes 1048592 | tf_op jit(solution)/shard_map/all_gather | solution.py:64
  260.0 2.8 copy.23
  262.7 2.5 broadcast_in_dim.41
  265.2 16.6 %while.21 = (s32[]{:T(128)}, f32[128,128,64]{1,2,0:T(8,128)}, s32[]{:T(128)}, s32[384]{0:T(512)S(1)}, s32[]{:T(128)}, /*index=5*/bf16[384,128,128]{2,1,0:T(8,128...) while((s32[]{:T(128)}, f32[128,128,64]{1,2,0:T(8,128)}, ...), condition=%wide.region_6.7_spmd, body=%wide.region_4.6_spmd.sunk | while | flops 135268160 | bytes 14686519 | solution.py:36
  265.2 0.7 compare_and_fusion.5
  266.0 0.1 compare_select_fusion.7
  266.0 3.7 gather_fusion.1
  269.8 3.0 fusion.35
  272.8 9.1 %scatter_fusion.1 = f32[128,128,64]{1,2,0:T(8,128)} fusion(f32[128,128,64]{1,2,0:T(8,128)} %get-tuple-element.302, s32[64]{0:T(128)S(1)} %get-tuple-element.251, f32[64,128,64]{1,2,0:T(8,128)S(1)} %fusion.35), kind=kCustom, calls=%fused_computation.3.clone.1 | custom fusion | flops 524288 | bytes 6291712 | tf_op jit(solution)/shard_map/while/body/scatter-add | solution.py:33
  281.9 4.4 copy_bitcast_fusion
  286.3 0.9 copy-done.1
  287.2 0.8 fusion.12
  288.1 159.8 %reduce-scatter.5.cloned.1.call-done = f32[1024,64]{0,1:T(8,128)} async-done(((f32[16384,64]{0,1:T(8,128)}), f32[1024,64]{0,1:T(8,128)}) %reduce-scatter.5.cloned.1.call-update) | async-done | bytes 262160 | tf_op jit(solution)/shard_map/reduce_scatter | solution.py:67
  447.9 1.6 convert_element_type.23
  449.5 138.3 %all-reduce.2.cloned.1.call-done = f32[64,256]{1,0:T(8,128)} async-done(((f32[64,256]{1,0:T(8,128)}), f32[64,256]{1,0:T(8,128)}) %all-reduce.2.cloned.1.call-update) | async-done | bytes 65552 | tf_op jit(solution)/shard_map/psum | solution.py:70
  587.8 1.5 copy.44
  (16 shorter events, 0.3 us)
Async XLA Ops:
  7.2 211.6 %copy-start = (bf16[64,256]{1,0:T(8,128)(2,1)S(1)}, bf16[64,256]{1,0:T(8,128)(2,1)}, u32[]{:S(2)}) copy-start(bf16[64,256]{1,0:T(8,128)(2,1)} %param.12) | copy-start | bytes 98308
  7.2 53.4 %all-gather.3.cloned.1.call-start = ((), (), s32[]{:S(2)}) async-start(), calls=%async_computation.2 | async-start | bytes 2228224 | tf_op jit(solution)/shard_map/all_gather | solution.py:55
  7.9 210.9 %reduce-scatter.3.cloned.1.call-start = ((), (), s32[]{:S(2)}) async-start(), calls=%async_computation.3 | async-start | bytes 2359296 | tf_op jit(solution)/shard_map/reduce_scatter | solution.py:57
  88.0 130.7 %copy-start.2 = (bf16[1024,256]{1,0:T(8,128)(2,1)S(1)}, bf16[1024,256]{1,0:T(8,128)(2,1)}, u32[]{:S(2)}) copy-start(bf16[1024,256]{1,0:T(8,128)(2,1)} %param.13) | copy-start | bytes 1572868
  88.1 171.9 %all-gather.5.cloned.1.call-start = ((), (), s32[]{:S(2)}) async-start(), calls=%async_computation.4 | async-start | bytes 1179648 | tf_op jit(solution)/shard_map/all_gather | solution.py:64
  222.2 225.7 %reduce-scatter.5.cloned.1.call-start = ((), (), s32[]{:S(2)}) async-start(), calls=%async_computation.5 | async-start | bytes 4456448 | tf_op jit(solution)/shard_map/reduce_scatter | solution.py:67
  286.3 0.9 copy-start.1
  286.3 301.5 %all-reduce.2.cloned.1.call-start = ((), (), s32[]{:S(2)}) async-start(), calls=%async_computation.6 | async-start | bytes 131072 | tf_op jit(solution)/shard_map/psum | solution.py:70
Sparse Core Ops, SparseCore 0:
  10.5 50.0 all-gather.2
  88.2 130.5 reduce-scatter.2
  222.3 37.6 all-gather.4
  286.4 161.4 reduce-scatter.4
  453.8 133.9 all-reduce.1
where the time goes:
time: 604 us; the launch traced here: 596 us
  waiting for transfers between devices  518 us (86%)
  local copies, waits for them, and re-layouts  29.5 us (5%)
  other arithmetic  22.9 us (4%)
  between operations  14.5 us (2%)
  matrix products  10.9 us (2%)
    reduce_scatter x1, waiting for transfers between devices, on_device(): lax.psum_scatter(grad_partial, 'row', scatter_dimension=0, tiled=True)  160 us
    psum x1, waiting for transfers between devices, on_device(): weight_grad = lax.psum(weight_part, ('row', 'col'))  138 us
    reduce_scatter x1, waiting for transfers between devices, on_device(): lax.psum_scatter(partial_value, 'col', scatter_dimension=0, tiled=True)  131 us
    all_gather x1, waiting for transfers between devices, on_device(): sources = lax.all_gather(features, 'row', axis=0, tiled=True)  50.6 us
    all_gather x1, waiting for transfers between devices, on_device(): grad_block = lax.all_gather(own_grad, 'col', axis=0, tiled=True)  37.7 us
    scatter-add x2, other arithmetic, advance(): return totals.at[target].add(product)  18.3 us
  transfers between devices with their start and end apart: 5, of which 5 were waited for; matrix products, arithmetic and copies ran while one was open for 1% of the time, Pallas kernels for 0%

commit v1 on v0

v1 whole, which is shorter than its diff:
```python
import functools

import jax
import jax.numpy as jnp
from jax import lax
from jax.experimental import pallas as pl
from jax.experimental.pallas import tpu as pltpu
from jax.sharding import Mesh, PartitionSpec as P

SIDE = 128
GROUP = 16
VMEM_LIMIT = 56 * 1024 * 1024
f32 = jnp.float32
bf16 = jnp.bfloat16

SMEM_SPEC = pl.BlockSpec(memory_space=pltpu.SMEM)
VMEM_SPEC = pl.BlockSpec(memory_space=pltpu.VMEM)
ANY_SPEC = pl.BlockSpec(memory_space=pl.ANY)


def run_tiles(live, targets, picks, values, tiles, total, sems, load, contract):
    groups = (live + GROUP - 1) // GROUP
    dump = total.shape[0] - 1

    def copy(group):
        here = pl.ds(group * GROUP, GROUP)
        return pltpu.make_async_copy(values.at[here], tiles.at[here], sems.at[group])

    def begin(group, carry):
        copy(group).start()
        return carry

    lax.fori_loop(0, groups, begin, 0)
    total[...] = jnp.zeros_like(total)

    def step(group, carry):
        copy(group).wait()
        products = []
        for i in range(GROUP):
            slot = group * GROUP + i
            products.append(
                lax.dot_general(
                    load(picks[0, 0, slot]), tiles[slot], contract, preferred_element_type=f32
                )
            )
        for i in range(GROUP):
            slot = group * GROUP + i
            target = jnp.where(slot < live, targets[0, 0, slot], dump)
            total[target] += products[i]
        return carry

    lax.fori_loop(0, groups, step, 0)


def forward_kernel(count, rows, cols, core, values, own, other, out, tiles, total, source, sems):
    mine = core[0]
    features = own.shape[1]
    for chip in range(own.shape[0]):
        for k in range(own.shape[2] // SIDE):
            lanes = slice(k * SIDE, (k + 1) * SIDE)
            source[chip, mine, k] = own[chip, :, lanes]
            source[chip, 1 - mine, k] = other[chip, :, lanes]

    def load(pick):
        return source[pick // 16, (pick // 8) % 2, pick % 8]

    run_tiles(count[0, 0], rows, cols, values, tiles, total, sems, load, (((1,), (1,)), ((), ())))
    per = out.shape[1] // features
    for tile in range(out.shape[0] * per):
        at = (tile % per) * features
        out[tile // per, at : at + features, :] = total[tile].astype(bf16)


def dense_kernel(parts, weight, cotangent, act, send):
    features = weight.shape[0]
    weight_part = jnp.zeros(weight.shape, f32)
    for k in range(act.shape[0] // SIDE):
        at = slice(k * features, (k + 1) * features)
        nodes = slice(k * SIDE, (k + 1) * SIDE)
        total = parts[0, at, :].astype(f32)
        for s in range(1, parts.shape[0]):
            total = total + parts[s, at, :].astype(f32)
        low = total.astype(bf16)
        pre = lax.dot_general(low, weight[...], (((0,), (0,)), ((), ())), preferred_element_type=f32)
        sigma = 1.0 / (1.0 + jnp.exp(-pre))
        act[nodes, :] = (pre * sigma).astype(bf16)
        grad = (cotangent[nodes, :].astype(f32) * sigma * (1.0 + pre * (1.0 - sigma))).astype(bf16)
        own = lax.dot_general(
            weight[...], grad, (((1,), (1,)), ((), ())), preferred_element_type=f32
        ).astype(bf16)
        for s in range(send.shape[0]):
            send[s, at, :] = own
        weight_part = weight_part + jnp.dot(low, grad, preferred_element_type=f32)
    base = parts.shape[1]
    low = weight_part.astype(bf16)
    for s in range(send.shape[0]):
        for k in range(weight.shape[1] // SIDE):
            send[s, base + k * features : base + (k + 1) * features, :] = low[:, k * SIDE : (k + 1) * SIDE]


def backward_kernel(count, rows, cols, core, values, grads, keep, give, tiles, total, sems):
    mine = core[0]
    chips, rows_each = keep.shape[0], keep.shape[1]
    extra = give.shape[0] - chips * rows_each
    features = rows_each // 8

    def load(pick):
        at = pl.multiple_of((pick % 8) * features, features)
        return grads[pick // 8, pl.ds(at, features), :]

    run_tiles(count[0, 0], cols, rows, values, tiles, total, sems, load, (((1,), (0,)), ((), ())))
    for chip in range(chips):
        for k in range(8):
            at = k * features
            keep[chip, at : at + features, :] = total[chip * 16 + mine * 8 + k]
            at = chip * rows_each + k * features
            give[at : at + features, :] = total[chip * 16 + (1 - mine) * 8 + k].astype(bf16)
    weight = grads[0, rows_each:, :].astype(f32)
    for s in range(1, grads.shape[0]):
        weight = weight + grads[s, rows_each:, :].astype(f32)
    give[chips * rows_each : chips * rows_each + extra, :] = weight.astype(bf16)


def pair_kernel(keep, give, got, send):
    chips, rows_each = keep.shape[0], keep.shape[1]
    for chip in range(chips):
        at = slice(chip * rows_each, (chip + 1) * rows_each)
        send[chip, :rows_each, :] = (keep[chip] + got[at, :].astype(f32)).astype(bf16)
    at = chips * rows_each
    weight = (give[at:, :].astype(f32) + got[at:, :].astype(f32)).astype(bf16)
    for chip in range(chips):
        send[chip, rows_each:, :] = weight


def last_kernel(parts, grad, weight_grad):
    features = grad.shape[0]
    for k in range(grad.shape[1] // SIDE):
        at = slice(k * features, (k + 1) * features)
        total = parts[0, at, :].astype(f32)
        for s in range(1, parts.shape[0]):
            total = total + parts[s, at, :].astype(f32)
        grad[:, k * SIDE : (k + 1) * SIDE] = total.astype(bf16)
    base = grad.shape[1] // SIDE * features
    for k in range(weight_grad.shape[1] // SIDE):
        at = slice(base + k * features, base + (k + 1) * features)
        total = parts[0, at, :].astype(f32)
        for s in range(1, parts.shape[0]):
            total = total + parts[s, at, :].astype(f32)
        weight_grad[:, k * SIDE : (k + 1) * SIDE] = total


def call(kernel, out_shape, in_specs, scratch=()):
    return pl.pallas_call(
        kernel,
        out_shape=out_shape,
        in_specs=in_specs,
        out_specs=jax.tree.map(lambda _: VMEM_SPEC, out_shape),
        scratch_shapes=scratch,
        compiler_params=pltpu.CompilerParams(vmem_limit_bytes=VMEM_LIMIT),
    )


def on_device(features, weight, cotangent, tile_values, tile_rows, tile_cols, tile_counts):
    nodes, width = features.shape
    hidden = weight.shape[1]
    slots = tile_values.shape[2]
    values = tile_values.reshape(slots, SIDE, SIDE)
    chips, cols = lax.axis_size("zy"), lax.axis_size("col")
    core = lax.axis_index("core").astype(jnp.int32).reshape(1)
    swap = [(0, 1), (1, 0)]
    shape = jax.ShapeDtypeStruct
    tiles_each = nodes // SIDE
    rows_each = tiles_each * width
    extra = hidden // SIDE * width

    own = lax.all_to_all(
        jnp.broadcast_to(features.T[None], (chips, width, nodes)), "zy", 0, 0, tiled=True
    )
    other = lax.ppermute(own, "core", swap)

    row_tiles, col_tiles = cols * tiles_each, 2 * chips * tiles_each
    tiles = pltpu.VMEM((slots, SIDE, SIDE), bf16)
    sems = pltpu.SemaphoreType.DMA((slots // GROUP,))
    partial = call(
        forward_kernel,
        shape((cols, rows_each, SIDE), bf16),
        [SMEM_SPEC] * 4 + [ANY_SPEC] + [VMEM_SPEC] * 2,
        [
            tiles,
            pltpu.VMEM((row_tiles + 1, width, SIDE), f32),
            pltpu.VMEM((chips, 2, tiles_each, width, SIDE), bf16),
            sems,
        ],
    )(tile_counts, tile_rows, tile_cols, core, values, own, other)

    parts = lax.all_to_all(partial, "col", 0, 0, tiled=True)
    activations, send = call(
        dense_kernel,
        (shape((nodes, hidden), bf16), shape((cols, rows_each + extra, SIDE), bf16)),
        [VMEM_SPEC] * 3,
    )(parts, weight, cotangent)

    grads = lax.all_to_all(send, "col", 0, 0, tiled=True)
    keep, give = call(
        backward_kernel,
        (shape((chips, rows_each, SIDE), f32), shape((chips * rows_each + extra, SIDE), bf16)),
        [SMEM_SPEC] * 4 + [ANY_SPEC] + [VMEM_SPEC],
        [tiles, pltpu.VMEM((col_tiles + 1, width, SIDE), f32), sems],
    )(tile_counts, tile_rows, tile_cols, core, values, grads)

    got = lax.ppermute(give, "core", swap)
    send = call(pair_kernel, shape((chips, rows_each + extra, SIDE), bf16), [VMEM_SPEC] * 3)(keep, give, got)
    parts = lax.all_to_all(send, "zy", 0, 0, tiled=True)
    grad, weight_grad = call(
        last_kernel,
        (shape((width, nodes), bf16), shape((width, hidden), f32)),
        [VMEM_SPEC],
    )(parts)
    return activations, grad.T, weight_grad


def solution(mesh):
    rows, cols = mesh.shape["row"], mesh.shape["col"]
    split = Mesh(mesh.devices.reshape(rows // 2, 2, cols), ("zy", "core", "col"))
    row = ("zy", "core")
    by_row = ("zy", "core", "col")
    by_col = ("col", "zy", "core")
    in_specs = (
        P(by_col, None),
        P(),
        P(by_row, None),
        P(row, "col", None, None, None),
        P(row, "col", None),
        P(row, "col", None),
        P(row, "col"),
    )
    out_specs = (P(by_row, None), P(by_col, None), P())
    return jax.shard_map(
        on_device, mesh=split, in_specs=in_specs, out_specs=out_specs, check_vma=False
    )
```

time: 604 us -> 137 us (0.23); the launches traced: 596 us -> 135 us
  waiting for transfers between devices: 518 us -> 4.55 us
  blocking collectives: 0 us -> 105 us
  local copies, waits for them, and re-layouts: 29.5 us -> 3.02 us
  other arithmetic: 22.9 us -> 0 us
  Pallas kernels: 0 us -> 19.2 us
  between operations: 14.5 us -> 1.31 us
  matrix products: 10.9 us -> 0 us
    reduce_scatter x2 -> x0, waiting for transfers between devices: 290 us -> none  [the longest x1 160 us: on_device(): lax.psum_scatter(grad_partial, 'row', scatter_dimension=0, tiled=True)]
    psum x1 -> x0, waiting for transfers between devices: 138 us -> none  [on_device(): weight_grad = lax.psum(weight_part, ('row', 'col'))]
    all_to_all x0 -> x4, blocking collectives: none -> 105 us  [the longest x1 29.9 us: on_device(): parts = lax.all_to_all(partial, 'col', 0, 0, tiled=True)]
    all_gather x2 -> x0, waiting for transfers between devices: 88.3 us -> none  [the longest x1 50.6 us: on_device(): sources = lax.all_gather(features, 'row', axis=0, tiled=True)]
    pallas_call x0 -> x5, Pallas kernels: none -> 19.2 us  [the longest x1 4.78 us: on_device(): call(backward_kernel, (shape((chips, rows_each, SIDE), f32), shape((chips...]
    scatter-add x2 -> x0, other arithmetic: 18.3 us -> none  [advance(): return totals.at[target].add(product)]
    dot_general x5 -> x0, matrix products: 10.9 us -> none  [the longest x1 3.73 us: advance(): jnp.einsum('tij,tjf->tif', block_values, picked, preferred_element_type=j...]
    gather x2 -> x0, local copies, waits for them, and re-layouts: 8.06 us -> none  [advance(): picked = tiled[pick]]
  transfers between devices with their start and end apart: 5 -> 2, of which waited for: 5 -> 2; matrix products, arithmetic and copies ran while one was open for 1% -> 0% of each run, Pallas kernels for 0% -> 0%
where the time goes in v1:
time: 137 us; the launch traced here: 135 us
  blocking collectives  105 us (77%)
  Pallas kernels  19.2 us (14%)
  waiting for transfers between devices  4.55 us (3%)
  local copies, waits for them, and re-layouts  3.02 us (2%)
  starting transfers between devices  2.33 us (2%)
    all_to_all x1, blocking collectives, on_device(): parts = lax.all_to_all(partial, 'col', 0, 0, tiled=True)  29.9 us
    all_to_all x1, blocking collectives, on_device(): parts = lax.all_to_all(send, 'zy', 0, 0, tiled=True)  26.9 us
    all_to_all x1, blocking collectives, on_device(): lax.all_to_all(jnp.broadcast_to(features.T[None], (chips, width, nodes)),...  25 us
    all_to_all x1, blocking collectives, on_device(): grads = lax.all_to_all(send, 'col', 0, 0, tiled=True)  23.1 us
    pallas_call x1, Pallas kernels, on_device(): call(backward_kernel, (shape((chips, rows_each, SIDE), f32), shape((chips...  4.78 us
    pallas_call x1, Pallas kernels, on_device(): call(forward_kernel, shape((cols, rows_each, SIDE), bf16), [SMEM_SPEC] *...  4.71 us
    pallas_call x1, Pallas kernels, on_device(): call(dense_kernel, (shape((nodes, hidden), bf16), shape((cols, rows_each...  4.11 us
    pallas_call x1, Pallas kernels, on_device(): call(pair_kernel, shape((chips, rows_each + extra, SIDE), bf16), [VMEM_SP...  3.44 us
  transfers between devices with their start and end apart: 2, of which 2 were waited for; matrix products, arithmetic and copies ran while one was open for 0% of the time, Pallas kernels for 0%

profile of v1, /device:TPU:0, one launch (start us, length us, event | category | flops | bytes accessed | tf_op | source)
XLA Modules:
  0.0 135.3 jit_solution(11041589992429982360)
XLA Ops:
  0.6 1.0 broadcast_in_dim.2
  1.7 25.0 %all_to_all.20.own = bf16[8,64,1024]{2,1,0:T(8,128)(2,1)S(1)} all-to-all(bf16[8,64,1024]{2,1,0:T(8,128)(2,1)S(1)} %broadcast_in_dim.2), channel_id=1, replica_groups=mesh['zy'=8,'core'=2,'col'=8] {'zy'}, dimensions={0} | all-to-all | bytes 2097152 | tf_op jit(solution)/shard_map/all_to_all | solution.py:176
  26.7 0.0 copy-start
  26.7 0.0 collective-permute-start
  27.3 2.0 %collective-permute-done.other = bf16[8,64,1024]{2,1,0:T(8,128)(2,1)S(1)} collective-permute-done((bf16[8,64,1024]{2,1,0:T(8,128)(2,1)S(1)}, bf16[8,64,1024]{2,1,0:T(8,128)(2,1)S(1)}, u32[]{:S(2)}, u32[]{:S(2)}) %collective-permute-start) | collective-permute-done | bytes 1048608 | tf_op jit(solution)/shard_map/ppermute | solution.py:179
  29.3 0.0 copy-start.2
  29.3 0.0 copy-done
  29.4 1.0 copy-done.2
  30.3 4.7 %shard_map.94 = bf16[8,512,128]{2,1,0:T(8,128)(2,1)} custom-call(s32[1,1]{1,0:T(1,128)S(6)} %copy.10.count, s32[1,1,384]{2,1,0:T(1,128)} %rows.3, s32[1,1,384]{2,1,0:T(1,128)} %cols.3, s32[1]{0:T(128)} %bitcast.core, bf16[384,128,128]{2,1,0:T(8,128)(2,1)} %bitcast.4, bf16[8,64,1024]{2,1,0:T(8,128)(2,1)} %copy-done, bf16[8,64,1024]{2,1,0:T(8,128)(2,1)} %copy-done.2), custom_call_target="tpu_custom_call" | custom-call | tf_op jit(solution)/shard_map/pallas_call | solution.py:184
  35.0 29.9 %all_to_all.21.parts = bf16[8,512,128]{2,1,0:T(8,128)(2,1)} all-to-all(bf16[8,512,128]{2,1,0:T(8,128)(2,1)} %shard_map.94), channel_id=1, replica_groups=mesh['zy'=8,'core'=2,'col'=8] {'col'}, dimensions={0} | all-to-all | bytes 2097152 | tf_op jit(solution)/shard_map/all_to_all | solution.py:196
  64.9 4.1 %shard_map.95 = (bf16[1024,256]{1,0:T(8,128)(2,1)}, bf16[8,640,128]{2,1,0:T(8,128)(2,1)}) custom-call(bf16[8,512,128]{2,1,0:T(8,128)(2,1)} %all_to_all.21.parts, bf16[64,256]{1,0:T(8,128)(2,1)} %weight.1, bf16[1024,256]{1,0:T(8,128)(2,1)} %cotangent.1), custom_call_target="tpu_custom_call" | custom-call | tf_op jit(solution)/shard_map/pallas_call | solution.py:197
  69.0 23.1 %all_to_all.22.grads = bf16[8,640,128]{2,1,0:T(8,128)(2,1)} all-to-all(bf16[8,640,128]{2,1,0:T(8,128)(2,1)} %get-tuple-element.10), channel_id=1, replica_groups=mesh['zy'=8,'core'=2,'col'=8] {'col'}, dimensions={0} | all-to-all | bytes 2621440 | tf_op jit(solution)/shard_map/all_to_all | solution.py:203
  92.2 4.8 %shard_map.96 = (f32[8,512,128]{2,1,0:T(8,128)}, bf16[4224,128]{1,0:T(8,128)(2,1)}) custom-call(s32[1,1]{1,0:T(1,128)S(6)} %copy.10.count, s32[1,1,384]{2,1,0:T(1,128)} %rows.3, s32[1,1,384]{2,1,0:T(1,128)} %cols.3, s32[1]{0:T(128)} %bitcast.core, bf16[384,128,128]{2,1,0:T(8,128)(2,1)} %bitcast.5, bf16[8,640,128]{2,1,0:T(8,128)(2,1)} %all_to_all.22.grads), custom_call_target="tpu_custom_call" | custom-call | tf_op jit(solution)/shard_map/pallas_call | solution.py:204
  97.0 2.3 %collective-permute-start.1 = (bf16[4224,128]{1,0:T(8,128)(2,1)}, bf16[4224,128]{1,0:T(8,128)(2,1)S(1)}, u32[]{:S(2)}, u32[]{:S(2)}) collective-permute-start(bf16[4224,128]{1,0:T(8,128)(2,1)} %get-tuple-element.12.give), channel_id=1, source_target_pairs={{0,8},{8,0},{1,9},{9,1},{2,10},{10,2},{3,11},{11,3},{4,12},{12,4},... | collective-permute-start | bytes 3244040 | tf_op jit(solution)/shard_map/ppermute | solution.py:211
  99.3 2.5 %collective-permute-done.1.got = bf16[4224,128]{1,0:T(8,128)(2,1)S(1)} collective-permute-done((bf16[4224,128]{1,0:T(8,128)(2,1)}, bf16[4224,128]{1,0:T(8,128)(2,1)S(1)}, u32[]{:S(2)}, u32[]{:S(2)}) %collective-permute-start.1) | collective-permute-done | bytes 1081376 | tf_op jit(solution)/shard_map/ppermute | solution.py:211
  101.8 0.0 copy-start.1
  101.8 1.0 copy-done.1
  102.8 3.4 %shard_map.97 = bf16[8,640,128]{2,1,0:T(8,128)(2,1)} custom-call(f32[8,512,128]{2,1,0:T(8,128)} %get-tuple-element.11.keep, bf16[4224,128]{1,0:T(8,128)(2,1)} %get-tuple-element.12.give, bf16[4224,128]{1,0:T(8,128)(2,1)} %copy-done.1), custom_call_target="tpu_custom_call" | custom-call | tf_op jit(solution)/shard_map/pallas_call | solution.py:212
  106.3 26.9 %all_to_all.23.parts = bf16[8,640,128]{2,1,0:T(8,128)(2,1)} all-to-all(bf16[8,640,128]{2,1,0:T(8,128)(2,1)} %shard_map.97), channel_id=1, replica_groups=mesh['zy'=8,'core'=2,'col'=8] {'zy'}, dimensions={0} | all-to-all | bytes 2621440 | tf_op jit(solution)/shard_map/all_to_all | solution.py:213
  133.2 2.1 %shard_map.98 = (bf16[64,1024]{1,0:T(8,128)(2,1)}, f32[64,256]{1,0:T(8,128)}) custom-call(bf16[8,640,128]{2,1,0:T(8,128)(2,1)} %all_to_all.23.parts), custom_call_target="tpu_custom_call" | custom-call | tf_op jit(solution)/shard_map/pallas_call | solution.py:214
Async XLA Ops:
  26.7 2.7 %copy-start = (bf16[8,64,1024]{2,1,0:T(8,128)(2,1)}, bf16[8,64,1024]{2,1,0:T(8,128)(2,1)S(1)}, u32[]{:S(2)}) copy-start(bf16[8,64,1024]{2,1,0:T(8,128)(2,1)S(1)} %all_to_all.20.own) | copy-start | bytes 3145732
  26.7 2.7 %collective-permute-start = (bf16[8,64,1024]{2,1,0:T(8,128)(2,1)S(1)}, bf16[8,64,1024]{2,1,0:T(8,128)(2,1)S(1)}, u32[]{:S(2)}, u32[]{:S(2)}) collective-permute-start(bf16[8,64,1024]{2,1,0:T(8,128)(2,1)S(1)} %all_to_all.20.own), channel_id=1, source_target_pairs={{0,8},{8,0},{1,9},{9,1},{2,10},{10,2},{3,11},{11,3},{4,12},{12,4},... | collective-permute-start | bytes 3145736 | tf_op jit(solution)/shard_map/ppermute | solution.py:179
  29.3 1.0 copy-start.2
  97.0 4.9 %collective-permute-start.1 = (bf16[4224,128]{1,0:T(8,128)(2,1)}, bf16[4224,128]{1,0:T(8,128)(2,1)S(1)}, u32[]{:S(2)}, u32[]{:S(2)}) collective-permute-start(bf16[4224,128]{1,0:T(8,128)(2,1)} %get-tuple-element.12.give), channel_id=1, source_target_pairs={{0,8},{8,0},{1,9},{9,1},{2,10},{10,2},{3,11},{11,3},{4,12},{12,4},... | collective-permute-start | bytes 3244040 | tf_op jit(solution)/shard_map/ppermute | solution.py:211
  101.8 1.0 copy-start.1

commit v2 on v1

--- a/solution.py
+++ b/solution.py
@@ -8,67 +8,49 @@
 from jax.sharding import Mesh, PartitionSpec as P
 
 SIDE = 128
-GROUP = 16
-VMEM_LIMIT = 56 * 1024 * 1024
+GROUP = 64
+MIB = 1024 * 1024
 f32 = jnp.float32
 bf16 = jnp.bfloat16
 
 SMEM_SPEC = pl.BlockSpec(memory_space=pltpu.SMEM)
 VMEM_SPEC = pl.BlockSpec(memory_space=pltpu.VMEM)
-ANY_SPEC = pl.BlockSpec(memory_space=pl.ANY)
-
-
-def run_tiles(live, targets, picks, values, tiles, total, sems, load, contract):
-    groups = (live + GROUP - 1) // GROUP
+
+
+def run_tiles(live, targets, values, total, product):
     dump = total.shape[0] - 1
-
-    def copy(group):
-        here = pl.ds(group * GROUP, GROUP)
-        return pltpu.make_async_copy(values.at[here], tiles.at[here], sems.at[group])
-
-    def begin(group, carry):
-        copy(group).start()
-        return carry
-
-    lax.fori_loop(0, groups, begin, 0)
     total[...] = jnp.zeros_like(total)
 
     def step(group, carry):
-        copy(group).wait()
-        products = []
-        for i in range(GROUP):
-            slot = group * GROUP + i
-            products.append(
-                lax.dot_general(
-                    load(picks[0, 0, slot]), tiles[slot], contract, preferred_element_type=f32
-                )
-            )
+        products = [product(group * GROUP + i) for i in range(GROUP)]
         for i in range(GROUP):
             slot = group * GROUP + i
             target = jnp.where(slot < live, targets[0, 0, slot], dump)
             total[target] += products[i]
         return carry
 
-    lax.fori_loop(0, groups, step, 0)
-
-
-def forward_kernel(count, rows, cols, core, values, own, other, out, tiles, total, source, sems):
+    lax.fori_loop(0, (live + GROUP - 1) // GROUP, step, 0)
+
+
+def forward_kernel(count, rows, cols, core, values, own, other, out, total, source):
     mine = core[0]
     features = own.shape[1]
     for chip in range(own.shape[0]):
         for k in range(own.shape[2] // SIDE):
             lanes = slice(k * SIDE, (k + 1) * SIDE)
-            source[chip, mine, k] = own[chip, :, lanes]
-            source[chip, 1 - mine, k] = other[chip, :, lanes]
-
-    def load(pick):
-        return source[pick // 16, (pick // 8) % 2, pick % 8]
-
-    run_tiles(count[0, 0], rows, cols, values, tiles, total, sems, load, (((1,), (1,)), ((), ())))
+            source[chip * 16 + mine * 8 + k] = own[chip, :, lanes]
+            source[chip * 16 + (1 - mine) * 8 + k] = other[chip, :, lanes]
+
+    def product(slot):
+        return lax.dot_general(
+            values[slot], source[cols[0, 0, slot]], (((1,), (1,)), ((), ())), preferred_element_type=f32
+        )
+
+    run_tiles(count[0, 0], rows, values, total, product)
     per = out.shape[1] // features
     for tile in range(out.shape[0] * per):
         at = (tile % per) * features
-        out[tile // per, at : at + features, :] = total[tile].astype(bf16)
+        out[tile // per, at : at + features, :] = total[tile].T.astype(bf16)
 
 
 def dense_kernel(parts, weight, cotangent, act, send):
@@ -98,17 +80,18 @@
             send[s, base + k * features : base + (k + 1) * features, :] = low[:, k * SIDE : (k + 1) * SIDE]
 
 
-def backward_kernel(count, rows, cols, core, values, grads, keep, give, tiles, total, sems):
+def backward_kernel(count, rows, cols, core, values, grads, keep, give, total):
     mine = core[0]
     chips, rows_each = keep.shape[0], keep.shape[1]
     extra = give.shape[0] - chips * rows_each
     features = rows_each // 8
 
-    def load(pick):
+    def product(slot):
+        pick = rows[0, 0, slot]
         at = pl.multiple_of((pick % 8) * features, features)
-        return grads[pick // 8, pl.ds(at, features), :]
-
-    run_tiles(count[0, 0], cols, rows, values, tiles, total, sems, load, (((1,), (0,)), ((), ())))
+        return jnp.dot(grads[pick // 8, pl.ds(at, features), :], values[slot], preferred_element_type=f32)
+
+    run_tiles(count[0, 0], cols, values, total, product)
     for chip in range(chips):
         for k in range(8):
             at = k * features
@@ -149,15 +132,16 @@
         weight_grad[:, k * SIDE : (k + 1) * SIDE] = total
 
 
-def call(kernel, out_shape, in_specs, scratch=()):
+def call(kernel, out_shape, scalars, arrays, scratch=(), limit=8):
+    arrays = [pltpu.with_memory_space_constraint(x, pltpu.VMEM) for x in arrays]
     return pl.pallas_call(
         kernel,
         out_shape=out_shape,
-        in_specs=in_specs,
+        in_specs=[SMEM_SPEC] * len(scalars) + [VMEM_SPEC] * len(arrays),
         out_specs=jax.tree.map(lambda _: VMEM_SPEC, out_shape),
         scratch_shapes=scratch,
-        compiler_params=pltpu.CompilerParams(vmem_limit_bytes=VMEM_LIMIT),
-    )
+        compiler_params=pltpu.CompilerParams(vmem_limit_bytes=limit * MIB),
+    )(*scalars, *arrays)
 
 
 def on_device(features, weight, cotangent, tile_values, tile_rows, tile_cols, tile_counts):
@@ -179,43 +163,43 @@
     other = lax.ppermute(own, "core", swap)
 
     row_tiles, col_tiles = cols * tiles_each, 2 * chips * tiles_each
-    tiles = pltpu.VMEM((slots, SIDE, SIDE), bf16)
-    sems = pltpu.SemaphoreType.DMA((slots // GROUP,))
+    scalars = (tile_counts, tile_rows, tile_cols, core)
     partial = call(
         forward_kernel,
         shape((cols, rows_each, SIDE), bf16),
-        [SMEM_SPEC] * 4 + [ANY_SPEC] + [VMEM_SPEC] * 2,
+        scalars,
+        (values, own, other),
         [
-            tiles,
-            pltpu.VMEM((row_tiles + 1, width, SIDE), f32),
-            pltpu.VMEM((chips, 2, tiles_each, width, SIDE), bf16),
-            sems,
+            pltpu.VMEM((row_tiles + 1, SIDE, width), f32),
+            pltpu.VMEM((col_tiles, width, SIDE), bf16),
         ],
-    )(tile_counts, tile_rows, tile_cols, core, values, own, other)
+        limit=12,
+    )
 
     parts = lax.all_to_all(partial, "col", 0, 0, tiled=True)
     activations, send = call(
         dense_kernel,
         (shape((nodes, hidden), bf16), shape((cols, rows_each + extra, SIDE), bf16)),
-        [VMEM_SPEC] * 3,
-    )(parts, weight, cotangent)
+        (),
+        (parts, weight, cotangent),
+    )
 
     grads = lax.all_to_all(send, "col", 0, 0, tiled=True)
     keep, give = call(
         backward_kernel,
         (shape((chips, rows_each, SIDE), f32), shape((chips * rows_each + extra, SIDE), bf16)),
-        [SMEM_SPEC] * 4 + [ANY_SPEC] + [VMEM_SPEC],
-        [tiles, pltpu.VMEM((col_tiles + 1, width, SIDE), f32), sems],
-    )(tile_counts, tile_rows, tile_cols, core, values, grads)
+        scalars,
+        (values, grads),
+        [pltpu.VMEM((col_tiles + 1, width, SIDE), f32)],
+        limit=12,
+    )
 
     got = lax.ppermute(give, "core", swap)
-    send = call(pair_kernel, shape((chips, rows_each + extra, SIDE), bf16), [VMEM_SPEC] * 3)(keep, give, got)
+    send = call(pair_kernel, shape((chips, rows_each + extra, SIDE), bf16), (), (keep, give, got))
     parts = lax.all_to_all(send, "zy", 0, 0, tiled=True)
     grad, weight_grad = call(
-        last_kernel,
-        (shape((width, nodes), bf16), shape((width, hidden), f32)),
-        [VMEM_SPEC],
-    )(parts)
+        last_kernel, (shape((width, nodes), bf16), shape((width, hidden), f32)), (), (parts,)
+    )
     return activations, grad.T, weight_grad
 
 

time: 137 us -> 116 us (0.85); the launches traced: 135 us -> 116 us
  Pallas kernels: 19.2 us -> 7.9 us
  blocking collectives: 105 us -> 96.2 us
  local copies, waits for them, and re-layouts: 3.02 us -> 5.62 us
  starting transfers between devices: 2.33 us -> 0.09 us
    pallas_call x5, Pallas kernels: 19.2 us -> 7.9 us  [call(): pl.pallas_call(kernel, out_shape=out_shape, in_specs=[SMEM_SPEC] * len(sc...]
    all_to_all x1, blocking collectives: 29.9 us -> 21.7 us  [on_device(): parts = lax.all_to_all(partial, 'col', 0, 0, tiled=True)]
    all_to_all x1, blocking collectives: 23.1 us -> 20.2 us  [on_device(): grads = lax.all_to_all(send, 'col', 0, 0, tiled=True)]
    unnamed x6 -> x10, local copies, waits for them, and re-layouts: 2 us -> 4.6 us
    all_to_all x1, blocking collectives: 26.9 us -> 29.2 us  [on_device(): parts = lax.all_to_all(send, 'zy', 0, 0, tiled=True)]
    ppermute x1, starting transfers between devices: 2.33 us -> 0.09 us  [on_device(): got = lax.ppermute(give, 'core', swap)]
where the time goes in v2:
time: 116 us
  blocking collectives  96.2 us (83%)
  Pallas kernels  7.9 us (7%)
  local copies, waits for them, and re-layouts  5.62 us (5%)
  waiting for transfers between devices  4.7 us (4%)
  between operations  1.35 us (1%)
    all_to_all x1, blocking collectives, on_device(): parts = lax.all_to_all(send, 'zy', 0, 0, tiled=True)  29.2 us
    all_to_all x1, blocking collectives, on_device(): lax.all_to_all(jnp.broadcast_to(features.T[None], (chips, width, nodes)),...  25.2 us
    all_to_all x1, blocking collectives, on_device(): parts = lax.all_to_all(partial, 'col', 0, 0, tiled=True)  21.7 us
    all_to_all x1, blocking collectives, on_device(): grads = lax.all_to_all(send, 'col', 0, 0, tiled=True)  20.2 us
    pallas_call x5, Pallas kernels, call(): pl.pallas_call(kernel, out_shape=out_shape, in_specs=[SMEM_SPEC] * len(sc...  7.9 us
    unnamed x10, local copies, waits for them, and re-layouts  4.6 us
    ppermute x1, waiting for transfers between devices, on_device(): got = lax.ppermute(give, 'core', swap)  2.69 us
  transfers between devices with their start and end apart: 2, of which 2 were waited for; matrix products, arithmetic and copies ran while one was open for 0% of the time, Pallas kernels for 0%

profile of v2, /device:TPU:0, one launch (start us, length us, event | category | flops | bytes accessed | tf_op | source)
XLA Modules:
  0.0 115.9 jit_solution(10256021493777257936)
XLA Ops:
  0.6 1.0 broadcast_in_dim.2
  1.7 0.0 copy-start.3
  1.7 0.0 copy-start.4
  1.7 25.2 %all_to_all.20.own = bf16[8,64,1024]{2,1,0:T(8,128)(2,1)S(1)} all-to-all(bf16[8,64,1024]{2,1,0:T(8,128)(2,1)S(1)} %broadcast_in_dim.2), channel_id=1, replica_groups=mesh['zy'=8,'core'=2,'col'=8] {'zy'}, dimensions={0} | all-to-all | bytes 2097152 | tf_op jit(solution)/shard_map/all_to_all | solution.py:160
  26.8 0.0 collective-permute-start
  27.5 2.0 %collective-permute-done.other = bf16[8,64,1024]{2,1,0:T(8,128)(2,1)S(1)} collective-permute-done((bf16[8,64,1024]{2,1,0:T(8,128)(2,1)S(1)}, bf16[8,64,1024]{2,1,0:T(8,128)(2,1)S(1)}, u32[]{:S(2)}, u32[]{:S(2)}) %collective-permute-start) | collective-permute-done | bytes 1048608 | tf_op jit(solution)/shard_map/ppermute | solution.py:163
  29.5 0.0 copy-done.3
  29.5 0.0 copy-done.4
  29.5 0.0 copy-start
  29.5 4.6 %copy-done = bf16[1,1,384,128,128]{4,3,2,1,0:T(8,128)(2,1)S(1)} copy-done((bf16[1,1,384,128,128]{4,3,2,1,0:T(8,128)(2,1)S(1)}, bf16[1,1,384,128,128]{4,3,2,1,0:T(8,128)(2,1)}, u32[]{:S(2)}) %copy-start) | copy-done | bytes 12582936
  34.1 2.6 %shard_map.94 = bf16[8,512,128]{2,1,0:T(8,128)(2,1)S(1)} custom-call(s32[1,1]{1,0:T(1,128)S(6)} %copy.10.count, s32[1,1,384]{2,1,0:T(1,128)S(1)} %copy-done.3, s32[1,1,384]{2,1,0:T(1,128)S(1)} %copy-done.4, s32[1]{0:T(128)} %bitcast.core, bf16[384,128,128]{2,1,0:T(8,128)(2,1)S(1)} %bitcast.4, bf16[8,64,1024]{2,1,0:T(8,128)(2,1)S(1)} %all_to_all.20.own, ...), custom_call_target="tpu_custom_call" | custom-call | tf_op jit(solution)/shard_map/pallas_call | solution.py:137
  36.7 0.0 copy-start.1
  36.7 0.0 copy-start.2
  36.7 21.7 %all_to_all.21.parts = bf16[8,512,128]{2,1,0:T(8,128)(2,1)S(1)} all-to-all(bf16[8,512,128]{2,1,0:T(8,128)(2,1)S(1)} %shard_map.94), channel_id=1, replica_groups=mesh['zy'=8,'core'=2,'col'=8] {'col'}, dimensions={0} | all-to-all | bytes 2097152 | tf_op jit(solution)/shard_map/all_to_all | solution.py:179
  58.4 0.0 copy-done.1
  58.4 0.0 copy-done.2
  58.4 2.3 %shard_map.95 = (bf16[1024,256]{1,0:T(8,128)(2,1)}, bf16[8,640,128]{2,1,0:T(8,128)(2,1)S(1)}) custom-call(bf16[8,512,128]{2,1,0:T(8,128)(2,1)S(1)} %all_to_all.21.parts, bf16[64,256]{1,0:T(8,128)(2,1)S(1)} %copy-done.2, bf16[1024,256]{1,0:T(8,128)(2,1)S(1)} %copy-done.1), custom_call_target="tpu_custom_call" | custom-call | tf_op jit(solution)/shard_map/pallas_call | solution.py:137
  60.7 20.2 %all_to_all.22.grads = bf16[8,640,128]{2,1,0:T(8,128)(2,1)S(1)} all-to-all(bf16[8,640,128]{2,1,0:T(8,128)(2,1)S(1)} %get-tuple-element.10), channel_id=1, replica_groups=mesh['zy'=8,'core'=2,'col'=8] {'col'}, dimensions={0} | all-to-all | bytes 2621440 | tf_op jit(solution)/shard_map/all_to_all | solution.py:187
  80.9 1.9 %shard_map.96 = (f32[8,512,128]{2,1,0:T(8,128)S(1)}, bf16[4224,128]{1,0:T(8,128)(2,1)S(1)}) custom-call(s32[1,1]{1,0:T(1,128)S(6)} %copy.10.count, s32[1,1,384]{2,1,0:T(1,128)S(1)} %copy-done.3, s32[1,1,384]{2,1,0:T(1,128)S(1)} %copy-done.4, s32[1]{0:T(128)} %bitcast.core, bf16[384,128,128]{2,1,0:T(8,128)(2,1)S(1)} %bitcast.5, ...), custom_call_target="tpu_custom_call" | custom-call | tf_op jit(solution)/shard_map/pallas_call | solution.py:137
  82.8 0.1 collective-permute-start.1
  82.9 2.7 %collective-permute-done.1.got = bf16[4224,128]{1,0:T(8,128)(2,1)S(1)} collective-permute-done((bf16[4224,128]{1,0:T(8,128)(2,1)S(1)}, bf16[4224,128]{1,0:T(8,128)(2,1)S(1)}, u32[]{:S(2)}, u32[]{:S(2)}) %collective-permute-start.1) | collective-permute-done | bytes 1081376 | tf_op jit(solution)/shard_map/ppermute | solution.py:197
  85.6 0.3 shard_map.97
  85.9 29.2 %all_to_all.23.parts = bf16[8,640,128]{2,1,0:T(8,128)(2,1)S(1)} all-to-all(bf16[8,640,128]{2,1,0:T(8,128)(2,1)S(1)} %shard_map.97), channel_id=1, replica_groups=mesh['zy'=8,'core'=2,'col'=8] {'zy'}, dimensions={0} | all-to-all | bytes 2621440 | tf_op jit(solution)/shard_map/all_to_all | solution.py:199
  115.1 0.8 shard_map.98
Async XLA Ops:
  1.7 27.8 %copy-start.3 = (s32[1,1,384]{2,1,0:T(1,128)S(1)}, s32[1,1,384]{2,1,0:T(1,128)}, u32[]{:S(2)}) copy-start(s32[1,1,384]{2,1,0:T(1,128)} %rows.3) | copy-start | bytes 4612
  1.7 27.8 %copy-start.4 = (s32[1,1,384]{2,1,0:T(1,128)S(1)}, s32[1,1,384]{2,1,0:T(1,128)}, u32[]{:S(2)}) copy-start(s32[1,1,384]{2,1,0:T(1,128)} %cols.3) | copy-start | bytes 4612
  26.8 2.7 %collective-permute-start = (bf16[8,64,1024]{2,1,0:T(8,128)(2,1)S(1)}, bf16[8,64,1024]{2,1,0:T(8,128)(2,1)S(1)}, u32[]{:S(2)}, u32[]{:S(2)}) collective-permute-start(bf16[8,64,1024]{2,1,0:T(8,128)(2,1)S(1)} %all_to_all.20.own), channel_id=1, source_target_pairs={{0,8},{8,0},{1,9},{9,1},{2,10},{10,2},{3,11},{11,3},{4,12},{12,4},... | collective-permute-start | bytes 3145736 | tf_op jit(solution)/shard_map/ppermute | solution.py:163
  29.5 4.6 %copy-start = (bf16[1,1,384,128,128]{4,3,2,1,0:T(8,128)(2,1)S(1)}, bf16[1,1,384,128,128]{4,3,2,1,0:T(8,128)(2,1)}, u32[]{:S(2)}) copy-start(bf16[1,1,384,128,128]{4,3,2,1,0:T(8,128)(2,1)} %param.10) | copy-start | bytes 37748740
  36.7 21.7 %copy-start.1 = (bf16[1024,256]{1,0:T(8,128)(2,1)S(1)}, bf16[1024,256]{1,0:T(8,128)(2,1)}, u32[]{:S(2)}) copy-start(bf16[1024,256]{1,0:T(8,128)(2,1)} %cotangent.1) | copy-start | bytes 1572868
  36.7 21.7 %copy-start.2 = (bf16[64,256]{1,0:T(8,128)(2,1)S(1)}, bf16[64,256]{1,0:T(8,128)(2,1)}, u32[]{:S(2)}) copy-start(bf16[64,256]{1,0:T(8,128)(2,1)} %weight.1) | copy-start | bytes 98308
  82.8 2.8 %collective-permute-start.1 = (bf16[4224,128]{1,0:T(8,128)(2,1)S(1)}, bf16[4224,128]{1,0:T(8,128)(2,1)S(1)}, u32[]{:S(2)}, u32[]{:S(2)}) collective-permute-start(bf16[4224,128]{1,0:T(8,128)(2,1)S(1)} %get-tuple-element.12.give), channel_id=1, source_target_pairs={{0,8},{8,0},{1,9},{9,1},{2,10},{10,2},{3,11},{11,3},{4,12},{12,4},... | collective-permute-start | bytes 3244040 | tf_op jit(solution)/shard_map/ppermute | solution.py:197

commit v3 on v2

--- a/solution.py
+++ b/solution.py
@@ -15,6 +15,11 @@
 
 SMEM_SPEC = pl.BlockSpec(memory_space=pltpu.SMEM)
 VMEM_SPEC = pl.BlockSpec(memory_space=pltpu.VMEM)
+
+
+def spread_kernel(features, out):
+    for chip in range(out.shape[0]):
+        out[chip] = features[...]
 
 
 def run_tiles(live, targets, values, total, product):
@@ -32,8 +37,8 @@
     lax.fori_loop(0, (live + GROUP - 1) // GROUP, step, 0)
 
 
-def forward_kernel(count, rows, cols, core, values, own, other, out, total, source):
-    mine = core[0]
+def forward_kernel(count, rows, cols, values, own, other, out, total, source):
+    mine = lax.axis_index("core")
     features = own.shape[1]
     for chip in range(own.shape[0]):
         for k in range(own.shape[2] // SIDE):
@@ -53,10 +58,10 @@
         out[tile // per, at : at + features, :] = total[tile].T.astype(bf16)
 
 
-def dense_kernel(parts, weight, cotangent, act, send):
+def dense_kernel(parts, weight, cotangent, pre_out, send):
     features = weight.shape[0]
     weight_part = jnp.zeros(weight.shape, f32)
-    for k in range(act.shape[0] // SIDE):
+    for k in range(pre_out.shape[0] // SIDE):
         at = slice(k * features, (k + 1) * features)
         nodes = slice(k * SIDE, (k + 1) * SIDE)
         total = parts[0, at, :].astype(f32)
@@ -65,7 +70,7 @@
         low = total.astype(bf16)
         pre = lax.dot_general(low, weight[...], (((0,), (0,)), ((), ())), preferred_element_type=f32)
         sigma = 1.0 / (1.0 + jnp.exp(-pre))
-        act[nodes, :] = (pre * sigma).astype(bf16)
+        pre_out[nodes, :] = pre
         grad = (cotangent[nodes, :].astype(f32) * sigma * (1.0 + pre * (1.0 - sigma))).astype(bf16)
         own = lax.dot_general(
             weight[...], grad, (((1,), (1,)), ((), ())), preferred_element_type=f32
@@ -80,35 +85,44 @@
             send[s, base + k * features : base + (k + 1) * features, :] = low[:, k * SIDE : (k + 1) * SIDE]
 
 
-def backward_kernel(count, rows, cols, core, values, grads, keep, give, total):
-    mine = core[0]
-    chips, rows_each = keep.shape[0], keep.shape[1]
-    extra = give.shape[0] - chips * rows_each
-    features = rows_each // 8
+def activation_kernel(pre, act):
+    for k in range(act.shape[0] // SIDE):
+        nodes = slice(k * SIDE, (k + 1) * SIDE)
+        x = pre[nodes, :]
+        act[nodes, :] = (x * (1.0 / (1.0 + jnp.exp(-x)))).astype(bf16)
+
+
+def backward_kernel(count, rows, cols, values, grads, total, give):
+    mine = lax.axis_index("core")
+    features = total.shape[1]
+    rows_each = 8 * features
 
     def product(slot):
         pick = rows[0, 0, slot]
-        at = pl.multiple_of((pick % 8) * features, features)
-        return jnp.dot(grads[pick // 8, pl.ds(at, features), :], values[slot], preferred_element_type=f32)
+        at = pl.multiple_of((pick & 7) * features, features)
+        return jnp.dot(grads[pick >> 3, pl.ds(at, features), :], values[slot], preferred_element_type=f32)
 
     run_tiles(count[0, 0], cols, values, total, product)
+    chips = total.shape[0] // 16
     for chip in range(chips):
         for k in range(8):
-            at = k * features
-            keep[chip, at : at + features, :] = total[chip * 16 + mine * 8 + k]
             at = chip * rows_each + k * features
             give[at : at + features, :] = total[chip * 16 + (1 - mine) * 8 + k].astype(bf16)
     weight = grads[0, rows_each:, :].astype(f32)
     for s in range(1, grads.shape[0]):
         weight = weight + grads[s, rows_each:, :].astype(f32)
-    give[chips * rows_each : chips * rows_each + extra, :] = weight.astype(bf16)
-
-
-def pair_kernel(keep, give, got, send):
-    chips, rows_each = keep.shape[0], keep.shape[1]
+    give[chips * rows_each :, :] = weight.astype(bf16)
+
+
+def pair_kernel(total, give, got, send):
+    mine = lax.axis_index("core")
+    chips, features = send.shape[0], total.shape[1]
+    rows_each = 8 * features
     for chip in range(chips):
-        at = slice(chip * rows_each, (chip + 1) * rows_each)
-        send[chip, :rows_each, :] = (keep[chip] + got[at, :].astype(f32)).astype(bf16)
+        for k in range(8):
+            at = chip * rows_each + k * features
+            pair = total[chip * 16 + mine * 8 + k] + got[at : at + features, :].astype(f32)
+            send[chip, k * features : (k + 1) * features, :] = pair.astype(bf16)
     at = chips * rows_each
     weight = (give[at:, :].astype(f32) + got[at:, :].astype(f32)).astype(bf16)
     for chip in range(chips):
@@ -132,7 +146,7 @@
         weight_grad[:, k * SIDE : (k + 1) * SIDE] = total
 
 
-def call(kernel, out_shape, scalars, arrays, scratch=(), limit=8):
+def call(kernel, out_shape, scalars, arrays, scratch=(), limit=8, cost=None):
     arrays = [pltpu.with_memory_space_constraint(x, pltpu.VMEM) for x in arrays]
     return pl.pallas_call(
         kernel,
@@ -140,6 +154,7 @@
         in_specs=[SMEM_SPEC] * len(scalars) + [VMEM_SPEC] * len(arrays),
         out_specs=jax.tree.map(lambda _: VMEM_SPEC, out_shape),
         scratch_shapes=scratch,
+        cost_estimate=cost,
         compiler_params=pltpu.CompilerParams(vmem_limit_bytes=limit * MIB),
     )(*scalars, *arrays)
 
@@ -150,20 +165,24 @@
     slots = tile_values.shape[2]
     values = tile_values.reshape(slots, SIDE, SIDE)
     chips, cols = lax.axis_size("zy"), lax.axis_size("col")
-    core = lax.axis_index("core").astype(jnp.int32).reshape(1)
     swap = [(0, 1), (1, 0)]
     shape = jax.ShapeDtypeStruct
     tiles_each = nodes // SIDE
     rows_each = tiles_each * width
     extra = hidden // SIDE * width
 
-    own = lax.all_to_all(
-        jnp.broadcast_to(features.T[None], (chips, width, nodes)), "zy", 0, 0, tiled=True
-    )
+    send = call(
+        spread_kernel,
+        shape((chips, width, nodes), bf16),
+        (),
+        (features.T,),
+        cost=pl.CostEstimate(flops=10**10, bytes_accessed=4 * 10**7, transcendentals=0),
+    )
+    own = lax.all_to_all(send, "zy", 0, 0, tiled=True)
     other = lax.ppermute(own, "core", swap)
 
     row_tiles, col_tiles = cols * tiles_each, 2 * chips * tiles_each
-    scalars = (tile_counts, tile_rows, tile_cols, core)
+    scalars = (tile_counts, tile_rows, tile_cols)
     partial = call(
         forward_kernel,
         shape((cols, rows_each, SIDE), bf16),
@@ -177,25 +196,32 @@
     )
 
     parts = lax.all_to_all(partial, "col", 0, 0, tiled=True)
-    activations, send = call(
+    pre, send = call(
         dense_kernel,
-        (shape((nodes, hidden), bf16), shape((cols, rows_each + extra, SIDE), bf16)),
+        (shape((nodes, hidden), f32), shape((cols, rows_each + extra, SIDE), bf16)),
         (),
         (parts, weight, cotangent),
     )
 
     grads = lax.all_to_all(send, "col", 0, 0, tiled=True)
-    keep, give = call(
+    total, give = call(
         backward_kernel,
-        (shape((chips, rows_each, SIDE), f32), shape((chips * rows_each + extra, SIDE), bf16)),
+        (
+            shape((col_tiles + 1, width, SIDE), f32),
+            shape((chips * rows_each + extra, SIDE), bf16),
+        ),
         scalars,
         (values, grads),
-        [pltpu.VMEM((col_tiles + 1, width, SIDE), f32)],
         limit=12,
     )
 
+    pre, give = lax.optimization_barrier((pre, give))
     got = lax.ppermute(give, "core", swap)
-    send = call(pair_kernel, shape((chips, rows_each + extra, SIDE), bf16), (), (keep, give, got))
+    activations = call(activation_kernel, shape((nodes, hidden), bf16), (), (pre,))
+    got, activations = lax.optimization_barrier((got, activations))
+    send = call(
+        pair_kernel, shape((chips, rows_each + extra, SIDE), bf16), (), (total, give, got)
+    )
     parts = lax.all_to_all(send, "zy", 0, 0, tiled=True)
     grad, weight_grad = call(
         last_kernel, (shape((width, nodes), bf16), shape((width, hidden), f32)), (), (parts,)

time: 116 us -> 110 us (0.948)
  blocking collectives: 96.2 us -> 88.3 us
  Pallas kernels: 7.9 us -> 15.2 us
  local copies, waits for them, and re-layouts: 5.62 us -> 1.08 us
    pallas_call x5 -> x7, Pallas kernels: 7.9 us -> 15.2 us  [call(): pl.pallas_call(kernel, out_shape=out_shape, in_specs=[SMEM_SPEC] * len(sc...]
    all_to_all x1, blocking collectives: 29.2 us -> 23 us  [on_device(): parts = lax.all_to_all(send, 'zy', 0, 0, tiled=True)]
    unnamed x10 -> x16, local copies, waits for them, and re-layouts: 4.6 us -> 1.08 us
    all_to_all x1, blocking collectives: 21.7 us -> 20 us  [on_device(): parts = lax.all_to_all(partial, 'col', 0, 0, tiled=True)]
  transfers between devices with their start and end apart: 2 -> 2, of which waited for: 2 -> 2; matrix products, arithmetic and copies ran while one was open for 0% -> 0% of each run, Pallas kernels for 0% -> 1%
where the time goes in v3:
time: 110 us
  blocking collectives  88.3 us (80%)
  Pallas kernels  15.2 us (14%)
  waiting for transfers between devices  3.62 us (3%)
  between operations  1.4 us (1%)
    all_to_all x1, blocking collectives, on_device(): own = lax.all_to_all(send, 'zy', 0, 0, tiled=True)  25.3 us
    all_to_all x1, blocking collectives, on_device(): parts = lax.all_to_all(send, 'zy', 0, 0, tiled=True)  23 us
    all_to_all x1, blocking collectives, on_device(): grads = lax.all_to_all(send, 'col', 0, 0, tiled=True)  20.1 us
    all_to_all x1, blocking collectives, on_device(): parts = lax.all_to_all(partial, 'col', 0, 0, tiled=True)  20 us
    pallas_call x7, Pallas kernels, call(): pl.pallas_call(kernel, out_shape=out_shape, in_specs=[SMEM_SPEC] * len(sc...  15.2 us
  transfers between devices with their start and end apart: 2, of which 2 were waited for; matrix products, arithmetic and copies ran while one was open for 0% of the time, Pallas kernels for 1%

profile of v3, /device:TPU:0, one launch (start us, length us, event | category | flops | bytes accessed | tf_op | source)
XLA Modules:
  0.0 109.8 jit_solution(15444994020500263377)
XLA Ops:
  0.6 0.0 slice-start
  0.6 0.0 copy-start.4
  0.7 1.0 copy-done.4
  1.7 0.0 slice-start.1
  1.7 0.0 slice-start.2
  1.7 0.1 shard_map.94
  1.8 0.0 copy-start.2
  1.8 0.0 copy-start.3
  1.8 25.3 %all_to_all.20.own = bf16[8,64,1024]{2,1,0:T(8,128)(2,1)S(1)} all-to-all(bf16[8,64,1024]{2,1,0:T(8,128)(2,1)S(1)} %shard_map.94), channel_id=1, replica_groups=mesh['zy'=8,'core'=2,'col'=8] {'zy'}, dimensions={0} | all-to-all | bytes 2097152 | tf_op jit(solution)/shard_map/all_to_all | solution.py:181
  27.1 0.0 collective-permute-start
  27.7 2.0 %collective-permute-done.other = bf16[8,64,1024]{2,1,0:T(8,128)(2,1)S(1)} collective-permute-done((bf16[8,64,1024]{2,1,0:T(8,128)(2,1)S(1)}, bf16[8,64,1024]{2,1,0:T(8,128)(2,1)S(1)}, u32[]{:S(2)}, u32[]{:S(2)}) %collective-permute-start) | collective-permute-done | bytes 1048608 | tf_op jit(solution)/shard_map/ppermute | solution.py:182
  29.7 0.0 slice-done
  29.8 0.0 slice-done.1
  29.8 0.0 slice-done.2
  29.8 0.0 copy-done.2
  29.8 0.0 copy-done.3
  29.8 6.4 %shard_map.95 = bf16[8,512,128]{2,1,0:T(8,128)(2,1)S(1)} custom-call(s32[1,1]{1,0:T(1,128)S(6)} %copy.10.count, s32[1,1,384]{2,1,0:T(1,128)S(1)} %copy-done.2, s32[1,1,384]{2,1,0:T(1,128)S(1)} %copy-done.3, bf16[384,128,128]{2,1,0:T(8,128)(2,1)S(1)} %bitcast.5, bf16[8,64,1024]{2,1,0:T(8,128)(2,1)S(1)} %all_to_all.20.own, ...), custom_call_target="tpu_custom_call" | custom-call | tf_op jit(solution)/shard_map/pallas_call | solution.py:151
  36.1 0.0 copy-start
  36.2 0.0 copy-start.1
  36.2 20.0 %all_to_all.21.parts = bf16[8,512,128]{2,1,0:T(8,128)(2,1)S(1)} all-to-all(bf16[8,512,128]{2,1,0:T(8,128)(2,1)S(1)} %shard_map.95), channel_id=1, replica_groups=mesh['zy'=8,'core'=2,'col'=8] {'col'}, dimensions={0} | all-to-all | bytes 2097152 | tf_op jit(solution)/shard_map/all_to_all | solution.py:198
  56.1 0.0 copy-done
  56.1 0.0 copy-done.1
  56.1 1.6 %shard_map.96 = (f32[1024,256]{1,0:T(8,128)S(1)}, bf16[8,640,128]{2,1,0:T(8,128)(2,1)S(1)}) custom-call(bf16[8,512,128]{2,1,0:T(8,128)(2,1)S(1)} %all_to_all.21.parts, bf16[64,256]{1,0:T(8,128)(2,1)S(1)} %copy-done.1, bf16[1024,256]{1,0:T(8,128)(2,1)S(1)} %copy-done), custom_call_target="tpu_custom_call" | custom-call | tf_op jit(solution)/shard_map/pallas_call | solution.py:151
  57.7 20.1 %all_to_all.22.grads = bf16[8,640,128]{2,1,0:T(8,128)(2,1)S(1)} all-to-all(bf16[8,640,128]{2,1,0:T(8,128)(2,1)S(1)} %get-tuple-element.14), channel_id=1, replica_groups=mesh['zy'=8,'core'=2,'col'=8] {'col'}, dimensions={0} | all-to-all | bytes 2621440 | tf_op jit(solution)/shard_map/all_to_all | solution.py:206
  77.8 5.1 %shard_map.97 = (f32[129,64,128]{2,1,0:T(8,128)S(1)}, bf16[4224,128]{1,0:T(8,128)(2,1)S(1)}) custom-call(s32[1,1]{1,0:T(1,128)S(6)} %copy.10.count, s32[1,1,384]{2,1,0:T(1,128)S(1)} %copy-done.2, s32[1,1,384]{2,1,0:T(1,128)S(1)} %copy-done.3, bf16[384,128,128]{2,1,0:T(8,128)(2,1)S(1)} %bitcast.6, bf16[8,640,128]{2,1,0:T(8,128)(2,1)S(1)} %all_to_all.22.grads), custom_call_target="tpu_custom_call" | custom-call | tf_op jit(solution)/shard_map/pallas_call | solution.py:151
  82.9 0.1 collective-permute-start.1
  83.0 1.1 shard_map.98
  84.1 1.6 %collective-permute-done.1.got = bf16[4224,128]{1,0:T(8,128)(2,1)S(1)} collective-permute-done((bf16[4224,128]{1,0:T(8,128)(2,1)S(1)}, bf16[4224,128]{1,0:T(8,128)(2,1)S(1)}, u32[]{:S(2)}, u32[]{:S(2)}) %collective-permute-start.1) | collective-permute-done | bytes 1081376 | tf_op jit(solution)/shard_map/ppermute | solution.py:219
  85.7 0.2 shard_map.99
  85.9 23.0 %all_to_all.23.parts = bf16[8,640,128]{2,1,0:T(8,128)(2,1)S(1)} all-to-all(bf16[8,640,128]{2,1,0:T(8,128)(2,1)S(1)} %shard_map.99), channel_id=1, replica_groups=mesh['zy'=8,'core'=2,'col'=8] {'zy'}, dimensions={0} | all-to-all | bytes 2621440 | tf_op jit(solution)/shard_map/all_to_all | solution.py:225
  109.0 0.8 shard_map.100
  (1 shorter events, 0.0 us)
Async XLA Ops:
  0.6 29.1 %slice-start = ((s8[12582912]{0:T(1024)(128)(4,1)}), s8[4194304]{0:T(1024)(128)(4,1)S(1)}, s32[]{:S(2)}) async-start(s8[12582912]{0:T(1024)(128)(4,1)} %bitcast.3), calls=%async_computation.4 | async-start | bytes 8388608
  0.6 1.1 copy-start.4
  1.7 28.1 %slice-start.1 = ((s8[12582912]{0:T(1024)(128)(4,1)}), s8[4194304]{0:T(1024)(128)(4,1)S(1)}, s32[]{:S(2)}) async-start(s8[12582912]{0:T(1024)(128)(4,1)} %bitcast.3), calls=%async_computation.5 | async-start | bytes 8388608
  1.7 28.1 %slice-start.2 = ((s8[12582912]{0:T(1024)(128)(4,1)}), s8[4194304]{0:T(1024)(128)(4,1)S(1)}, s32[]{:S(2)}) async-start(s8[12582912]{0:T(1024)(128)(4,1)} %bitcast.3), calls=%async_computation.6 | async-start | bytes 8388608
  1.8 28.0 %copy-start.2 = (s32[1,1,384]{2,1,0:T(1,128)S(1)}, s32[1,1,384]{2,1,0:T(1,128)}, u32[]{:S(2)}) copy-start(s32[1,1,384]{2,1,0:T(1,128)} %rows.3) | copy-start | bytes 4612
  1.8 28.0 %copy-start.3 = (s32[1,1,384]{2,1,0:T(1,128)S(1)}, s32[1,1,384]{2,1,0:T(1,128)}, u32[]{:S(2)}) copy-start(s32[1,1,384]{2,1,0:T(1,128)} %cols.3) | copy-start | bytes 4612
  27.1 2.7 %collective-permute-start = (bf16[8,64,1024]{2,1,0:T(8,128)(2,1)S(1)}, bf16[8,64,1024]{2,1,0:T(8,128)(2,1)S(1)}, u32[]{:S(2)}, u32[]{:S(2)}) collective-permute-start(bf16[8,64,1024]{2,1,0:T(8,128)(2,1)S(1)} %all_to_all.20.own), channel_id=1, source_target_pairs={{0,8},{8,0},{1,9},{9,1},{2,10},{10,2},{3,11},{11,3},{4,12},{12,4},... | collective-permute-start | bytes 3145736 | tf_op jit(solution)/shard_map/ppermute | solution.py:182
  36.1 20.0 %copy-start = (bf16[1024,256]{1,0:T(8,128)(2,1)S(1)}, bf16[1024,256]{1,0:T(8,128)(2,1)}, u32[]{:S(2)}) copy-start(bf16[1024,256]{1,0:T(8,128)(2,1)} %cotangent.1) | copy-start | bytes 1572868
  36.2 20.0 %copy-start.1 = (bf16[64,256]{1,0:T(8,128)(2,1)S(1)}, bf16[64,256]{1,0:T(8,128)(2,1)}, u32[]{:S(2)}) copy-start(bf16[64,256]{1,0:T(8,128)(2,1)} %weight.1) | copy-start | bytes 98308
  82.9 2.8 %collective-permute-start.1 = (bf16[4224,128]{1,0:T(8,128)(2,1)S(1)}, bf16[4224,128]{1,0:T(8,128)(2,1)S(1)}, u32[]{:S(2)}, u32[]{:S(2)}) collective-permute-start(bf16[4224,128]{1,0:T(8,128)(2,1)S(1)} %get-tuple-element.16.give), channel_id=1, source_target_pairs={{0,8},{8,0},{1,9},{9,1},{2,10},{10,2},{3,11},{11,3},{4,12},{12,4},... | collective-permute-start | bytes 3244040 | tf_op jit(solution)/shard_map/ppermute | solution.py:219

commit v4 on v3

--- a/solution.py
+++ b/solution.py
@@ -8,7 +8,8 @@
 from jax.sharding import Mesh, PartitionSpec as P
 
 SIDE = 128
-GROUP = 64
+GROUP = 192
+LAG = 8
 MIB = 1024 * 1024
 f32 = jnp.float32
 bf16 = jnp.bfloat16
@@ -27,11 +28,14 @@
     total[...] = jnp.zeros_like(total)
 
     def step(group, carry):
-        products = [product(group * GROUP + i) for i in range(GROUP)]
-        for i in range(GROUP):
-            slot = group * GROUP + i
-            target = jnp.where(slot < live, targets[0, 0, slot], dump)
-            total[target] += products[i]
+        products = []
+        for i in range(GROUP + LAG):
+            if i < GROUP:
+                products.append(product(group * GROUP + i))
+            if i >= LAG:
+                slot = group * GROUP + i - LAG
+                target = jnp.where(slot < live, targets[0, 0, slot], dump)
+                total[target] += products[i - LAG]
         return carry
 
     lax.fori_loop(0, (live + GROUP - 1) // GROUP, step, 0)
@@ -192,7 +196,7 @@
             pltpu.VMEM((row_tiles + 1, SIDE, width), f32),
             pltpu.VMEM((col_tiles, width, SIDE), bf16),
         ],
-        limit=12,
+        limit=20,
     )
 
     parts = lax.all_to_all(partial, "col", 0, 0, tiled=True)
@@ -212,7 +216,7 @@
         ),
         scalars,
         (values, grads),
-        limit=12,
+        limit=20,
     )
 
     pre, give = lax.optimization_barrier((pre, give))

time: 110 us -> 109 us (level)
  Pallas kernels: 15.2 us -> 10.4 us
  blocking collectives: 88.3 us -> 91.6 us
    pallas_call x7, Pallas kernels: 15.2 us -> 10.4 us  [call(): pl.pallas_call(kernel, out_shape=out_shape, in_specs=[SMEM_SPEC] * len(sc...]
    all_to_all x1, blocking collectives: 20 us -> 21.8 us  [on_device(): parts = lax.all_to_all(partial, 'col', 0, 0, tiled=True)]
    all_to_all x1, blocking collectives: 20.1 us -> 21.5 us  [on_device(): grads = lax.all_to_all(send, 'col', 0, 0, tiled=True)]
where the time goes in v4:
time: 109 us; the launch traced here: 108 us
  blocking collectives  91.6 us (84%)
  Pallas kernels  10.4 us (10%)
  waiting for transfers between devices  3.62 us (3%)
  between operations  1.4 us (1%)
    all_to_all x1, blocking collectives, on_device(): own = lax.all_to_all(send, 'zy', 0, 0, tiled=True)  25.3 us
    all_to_all x1, blocking collectives, on_device(): parts = lax.all_to_all(send, 'zy', 0, 0, tiled=True)  23 us
    all_to_all x1, blocking collectives, on_device(): parts = lax.all_to_all(partial, 'col', 0, 0, tiled=True)  21.8 us
    all_to_all x1, blocking collectives, on_device(): grads = lax.all_to_all(send, 'col', 0, 0, tiled=True)  21.5 us
    pallas_call x7, Pallas kernels, call(): pl.pallas_call(kernel, out_shape=out_shape, in_specs=[SMEM_SPEC] * len(sc...  10.4 us
  transfers between devices with their start and end apart: 2, of which 2 were waited for; matrix products, arithmetic and copies ran while one was open for 0% of the time, Pallas kernels for 1%

profile of v4, /device:TPU:0, one launch (start us, length us, event | category | flops | bytes accessed | tf_op | source)
XLA Modules:
  0.0 108.1 jit_solution(10189402784581334708)
XLA Ops:
  0.6 0.0 slice-start
  0.6 0.0 copy-start.4
  0.7 1.0 copy-done.4
  1.7 0.0 slice-start.1
  1.7 0.0 slice-start.2
  1.7 0.1 shard_map.94
  1.8 0.0 copy-start.2
  1.8 0.0 copy-start.3
  1.8 25.3 %all_to_all.20.own = bf16[8,64,1024]{2,1,0:T(8,128)(2,1)S(1)} all-to-all(bf16[8,64,1024]{2,1,0:T(8,128)(2,1)S(1)} %shard_map.94), channel_id=1, replica_groups=mesh['zy'=8,'core'=2,'col'=8] {'zy'}, dimensions={0} | all-to-all | bytes 2097152 | tf_op jit(solution)/shard_map/all_to_all | solution.py:185
  27.1 0.0 collective-permute-start
  27.7 2.0 %collective-permute-done.other = bf16[8,64,1024]{2,1,0:T(8,128)(2,1)S(1)} collective-permute-done((bf16[8,64,1024]{2,1,0:T(8,128)(2,1)S(1)}, bf16[8,64,1024]{2,1,0:T(8,128)(2,1)S(1)}, u32[]{:S(2)}, u32[]{:S(2)}) %collective-permute-start) | collective-permute-done | bytes 1048608 | tf_op jit(solution)/shard_map/ppermute | solution.py:186
  29.7 0.0 slice-done
  29.8 0.0 slice-done.1
  29.8 0.0 slice-done.2
  29.8 0.0 copy-done.2
  29.8 0.0 copy-done.3
  29.8 3.8 %shard_map.95 = bf16[8,512,128]{2,1,0:T(8,128)(2,1)S(1)} custom-call(s32[1,1]{1,0:T(1,128)S(6)} %copy.10.count, s32[1,1,384]{2,1,0:T(1,128)S(1)} %copy-done.2, s32[1,1,384]{2,1,0:T(1,128)S(1)} %copy-done.3, bf16[384,128,128]{2,1,0:T(8,128)(2,1)S(1)} %bitcast.5, bf16[8,64,1024]{2,1,0:T(8,128)(2,1)S(1)} %all_to_all.20.own, ...), custom_call_target="tpu_custom_call" | custom-call | tf_op jit(solution)/shard_map/pallas_call | solution.py:155
  33.6 0.0 copy-start
  33.6 0.0 copy-start.1
  33.6 21.8 %all_to_all.21.parts = bf16[8,512,128]{2,1,0:T(8,128)(2,1)S(1)} all-to-all(bf16[8,512,128]{2,1,0:T(8,128)(2,1)S(1)} %shard_map.95), channel_id=1, replica_groups=mesh['zy'=8,'core'=2,'col'=8] {'col'}, dimensions={0} | all-to-all | bytes 2097152 | tf_op jit(solution)/shard_map/all_to_all | solution.py:202
  55.4 0.0 copy-done
  55.4 0.0 copy-done.1
  55.4 1.6 %shard_map.96 = (f32[1024,256]{1,0:T(8,128)S(1)}, bf16[8,640,128]{2,1,0:T(8,128)(2,1)S(1)}) custom-call(bf16[8,512,128]{2,1,0:T(8,128)(2,1)S(1)} %all_to_all.21.parts, bf16[64,256]{1,0:T(8,128)(2,1)S(1)} %copy-done.1, bf16[1024,256]{1,0:T(8,128)(2,1)S(1)} %copy-done), custom_call_target="tpu_custom_call" | custom-call | tf_op jit(solution)/shard_map/pallas_call | solution.py:155
  57.0 21.5 %all_to_all.22.grads = bf16[8,640,128]{2,1,0:T(8,128)(2,1)S(1)} all-to-all(bf16[8,640,128]{2,1,0:T(8,128)(2,1)S(1)} %get-tuple-element.14), channel_id=1, replica_groups=mesh['zy'=8,'core'=2,'col'=8] {'col'}, dimensions={0} | all-to-all | bytes 2621440 | tf_op jit(solution)/shard_map/all_to_all | solution.py:210
  78.5 2.8 %shard_map.97 = (f32[129,64,128]{2,1,0:T(8,128)S(1)}, bf16[4224,128]{1,0:T(8,128)(2,1)S(1)}) custom-call(s32[1,1]{1,0:T(1,128)S(6)} %copy.10.count, s32[1,1,384]{2,1,0:T(1,128)S(1)} %copy-done.2, s32[1,1,384]{2,1,0:T(1,128)S(1)} %copy-done.3, bf16[384,128,128]{2,1,0:T(8,128)(2,1)S(1)} %bitcast.6, bf16[8,640,128]{2,1,0:T(8,128)(2,1)S(1)} %all_to_all.22.grads), custom_call_target="tpu_custom_call" | custom-call | tf_op jit(solution)/shard_map/pallas_call | solution.py:155
  81.3 0.1 collective-permute-start.1
  81.4 1.1 shard_map.98
  82.4 1.6 %collective-permute-done.1.got = bf16[4224,128]{1,0:T(8,128)(2,1)S(1)} collective-permute-done((bf16[4224,128]{1,0:T(8,128)(2,1)S(1)}, bf16[4224,128]{1,0:T(8,128)(2,1)S(1)}, u32[]{:S(2)}, u32[]{:S(2)}) %collective-permute-start.1) | collective-permute-done | bytes 1081376 | tf_op jit(solution)/shard_map/ppermute | solution.py:223
  84.1 0.2 shard_map.99
  84.3 23.0 %all_to_all.23.parts = bf16[8,640,128]{2,1,0:T(8,128)(2,1)S(1)} all-to-all(bf16[8,640,128]{2,1,0:T(8,128)(2,1)S(1)} %shard_map.99), channel_id=1, replica_groups=mesh['zy'=8,'core'=2,'col'=8] {'zy'}, dimensions={0} | all-to-all | bytes 2621440 | tf_op jit(solution)/shard_map/all_to_all | solution.py:229
  107.3 0.8 shard_map.100
  (1 shorter events, 0.0 us)
Async XLA Ops:
  0.6 29.1 %slice-start = ((s8[12582912]{0:T(1024)(128)(4,1)}), s8[4194304]{0:T(1024)(128)(4,1)S(1)}, s32[]{:S(2)}) async-start(s8[12582912]{0:T(1024)(128)(4,1)} %bitcast.3), calls=%async_computation.4 | async-start | bytes 8388608
  0.6 1.1 copy-start.4
  1.7 28.1 %slice-start.1 = ((s8[12582912]{0:T(1024)(128)(4,1)}), s8[4194304]{0:T(1024)(128)(4,1)S(1)}, s32[]{:S(2)}) async-start(s8[12582912]{0:T(1024)(128)(4,1)} %bitcast.3), calls=%async_computation.5 | async-start | bytes 8388608
  1.7 28.1 %slice-start.2 = ((s8[12582912]{0:T(1024)(128)(4,1)}), s8[4194304]{0:T(1024)(128)(4,1)S(1)}, s32[]{:S(2)}) async-start(s8[12582912]{0:T(1024)(128)(4,1)} %bitcast.3), calls=%async_computation.6 | async-start | bytes 8388608
  1.8 28.0 %copy-start.2 = (s32[1,1,384]{2,1,0:T(1,128)S(1)}, s32[1,1,384]{2,1,0:T(1,128)}, u32[]{:S(2)}) copy-start(s32[1,1,384]{2,1,0:T(1,128)} %rows.3) | copy-start | bytes 4612
  1.8 28.0 %copy-start.3 = (s32[1,1,384]{2,1,0:T(1,128)S(1)}, s32[1,1,384]{2,1,0:T(1,128)}, u32[]{:S(2)}) copy-start(s32[1,1,384]{2,1,0:T(1,128)} %cols.3) | copy-start | bytes 4612
  27.1 2.7 %collective-permute-start = (bf16[8,64,1024]{2,1,0:T(8,128)(2,1)S(1)}, bf16[8,64,1024]{2,1,0:T(8,128)(2,1)S(1)}, u32[]{:S(2)}, u32[]{:S(2)}) collective-permute-start(bf16[8,64,1024]{2,1,0:T(8,128)(2,1)S(1)} %all_to_all.20.own), channel_id=1, source_target_pairs={{0,8},{8,0},{1,9},{9,1},{2,10},{10,2},{3,11},{11,3},{4,12},{12,4},... | collective-permute-start | bytes 3145736 | tf_op jit(solution)/shard_map/ppermute | solution.py:186
  33.6 21.8 %copy-start = (bf16[1024,256]{1,0:T(8,128)(2,1)S(1)}, bf16[1024,256]{1,0:T(8,128)(2,1)}, u32[]{:S(2)}) copy-start(bf16[1024,256]{1,0:T(8,128)(2,1)} %cotangent.1) | copy-start | bytes 1572868
  33.6 21.8 %copy-start.1 = (bf16[64,256]{1,0:T(8,128)(2,1)S(1)}, bf16[64,256]{1,0:T(8,128)(2,1)}, u32[]{:S(2)}) copy-start(bf16[64,256]{1,0:T(8,128)(2,1)} %weight.1) | copy-start | bytes 98308
  81.3 2.8 %collective-permute-start.1 = (bf16[4224,128]{1,0:T(8,128)(2,1)S(1)}, bf16[4224,128]{1,0:T(8,128)(2,1)S(1)}, u32[]{:S(2)}, u32[]{:S(2)}) collective-permute-start(bf16[4224,128]{1,0:T(8,128)(2,1)S(1)} %get-tuple-element.16.give), channel_id=1, source_target_pairs={{0,8},{8,0},{1,9},{9,1},{2,10},{10,2},{3,11},{11,3},{4,12},{12,4},... | collective-permute-start | bytes 3244040 | tf_op jit(solution)/shard_map/ppermute | solution.py:223

commit v5 on v4

--- a/solution.py
+++ b/solution.py
@@ -56,10 +56,11 @@
         )
 
     run_tiles(count[0, 0], rows, values, total, product)
-    per = out.shape[1] // features
-    for tile in range(out.shape[0] * per):
-        at = (tile % per) * features
-        out[tile // per, at : at + features, :] = total[tile].T.astype(bf16)
+    per = out.shape[1] // SIDE
+    for pair in range(out.shape[0] * per):
+        at = (pair % per) * SIDE
+        both = jnp.concatenate([total[2 * pair].astype(bf16), total[2 * pair + 1].astype(bf16)], axis=1)
+        out[pair // per, at : at + SIDE, :] = both
 
 
 def dense_kernel(parts, weight, cotangent, pre_out, send):
@@ -68,11 +69,14 @@
     for k in range(pre_out.shape[0] // SIDE):
         at = slice(k * features, (k + 1) * features)
         nodes = slice(k * SIDE, (k + 1) * SIDE)
-        total = parts[0, at, :].astype(f32)
-        for s in range(1, parts.shape[0]):
-            total = total + parts[s, at, :].astype(f32)
-        low = total.astype(bf16)
-        pre = lax.dot_general(low, weight[...], (((0,), (0,)), ((), ())), preferred_element_type=f32)
+        if k % 2 == 0:
+            pair = slice(k // 2 * SIDE, (k // 2 + 1) * SIDE)
+            total = parts[0, pair, :].astype(f32)
+            for s in range(1, parts.shape[0]):
+                total = total + parts[s, pair, :].astype(f32)
+            both = total.astype(bf16)
+        low = both[:, (k % 2) * features : (k % 2 + 1) * features]
+        pre = jnp.dot(low, weight[...], preferred_element_type=f32)
         sigma = 1.0 / (1.0 + jnp.exp(-pre))
         pre_out[nodes, :] = pre
         grad = (cotangent[nodes, :].astype(f32) * sigma * (1.0 + pre * (1.0 - sigma))).astype(bf16)
@@ -81,7 +85,9 @@
         ).astype(bf16)
         for s in range(send.shape[0]):
             send[s, at, :] = own
-        weight_part = weight_part + jnp.dot(low, grad, preferred_element_type=f32)
+        weight_part = weight_part + lax.dot_general(
+            low, grad, (((0,), (0,)), ((), ())), preferred_element_type=f32
+        )
     base = parts.shape[1]
     low = weight_part.astype(bf16)
     for s in range(send.shape[0]):

time: 109 us -> 109 us (level)
  blocking collectives: 91.6 us -> 92.8 us
    all_to_all x1, blocking collectives: 23 us -> 25 us  [on_device(): parts = lax.all_to_all(send, 'zy', 0, 0, tiled=True)]
    all_to_all x1, blocking collectives: 21.5 us -> 20.3 us  [on_device(): grads = lax.all_to_all(send, 'col', 0, 0, tiled=True)]
where the time goes in v5:
time: 109 us
  blocking collectives  92.8 us (85%)
  Pallas kernels  9.95 us (9%)
  waiting for transfers between devices  3.5 us (3%)
  between operations  1.39 us (1%)
    all_to_all x1, blocking collectives, on_device(): own = lax.all_to_all(send, 'zy', 0, 0, tiled=True)  25.3 us
    all_to_all x1, blocking collectives, on_device(): parts = lax.all_to_all(send, 'zy', 0, 0, tiled=True)  25 us
    all_to_all x1, blocking collectives, on_device(): parts = lax.all_to_all(partial, 'col', 0, 0, tiled=True)  22.2 us
    all_to_all x1, blocking collectives, on_device(): grads = lax.all_to_all(send, 'col', 0, 0, tiled=True)  20.3 us
    pallas_call x7, Pallas kernels, call(): pl.pallas_call(kernel, out_shape=out_shape, in_specs=[SMEM_SPEC] * len(sc...  9.95 us
  transfers between devices with their start and end apart: 2, of which 2 were waited for; matrix products, arithmetic and copies ran while one was open for 0% of the time, Pallas kernels for 1%

profile of v5, /device:TPU:0, one launch (start us, length us, event | category | flops | bytes accessed | tf_op | source)
XLA Modules:
  0.0 108.9 jit_solution(3598822045250132326)
XLA Ops:
  0.6 0.0 slice-start
  0.6 0.0 copy-start.4
  0.7 1.0 copy-done.4
  1.7 0.0 slice-start.1
  1.7 0.0 slice-start.2
  1.7 0.1 shard_map.94
  1.8 0.0 copy-start.2
  1.8 0.0 copy-start.3
  1.8 25.3 %all_to_all.20.own = bf16[8,64,1024]{2,1,0:T(8,128)(2,1)S(1)} all-to-all(bf16[8,64,1024]{2,1,0:T(8,128)(2,1)S(1)} %shard_map.94), channel_id=1, replica_groups=mesh['zy'=8,'core'=2,'col'=8] {'zy'}, dimensions={0} | all-to-all | bytes 2097152 | tf_op jit(solution)/shard_map/all_to_all | solution.py:191
  27.1 0.0 collective-permute-start
  27.7 2.0 %collective-permute-done.other = bf16[8,64,1024]{2,1,0:T(8,128)(2,1)S(1)} collective-permute-done((bf16[8,64,1024]{2,1,0:T(8,128)(2,1)S(1)}, bf16[8,64,1024]{2,1,0:T(8,128)(2,1)S(1)}, u32[]{:S(2)}, u32[]{:S(2)}) %collective-permute-start) | collective-permute-done | bytes 1048608 | tf_op jit(solution)/shard_map/ppermute | solution.py:192
  29.7 0.0 slice-done
  29.8 0.0 slice-done.1
  29.8 0.0 slice-done.2
  29.8 0.0 copy-done.2
  29.8 0.0 copy-done.3
  29.8 3.5 %shard_map.95 = bf16[8,512,128]{2,1,0:T(8,128)(2,1)S(1)} custom-call(s32[1,1]{1,0:T(1,128)S(6)} %copy.10.count, s32[1,1,384]{2,1,0:T(1,128)S(1)} %copy-done.2, s32[1,1,384]{2,1,0:T(1,128)S(1)} %copy-done.3, bf16[384,128,128]{2,1,0:T(8,128)(2,1)S(1)} %bitcast.5, bf16[8,64,1024]{2,1,0:T(8,128)(2,1)S(1)} %all_to_all.20.own, ...), custom_call_target="tpu_custom_call" | custom-call | tf_op jit(solution)/shard_map/pallas_call | solution.py:161
  33.3 0.0 copy-start
  33.3 0.0 copy-start.1
  33.3 22.2 %all_to_all.21.parts = bf16[8,512,128]{2,1,0:T(8,128)(2,1)S(1)} all-to-all(bf16[8,512,128]{2,1,0:T(8,128)(2,1)S(1)} %shard_map.95), channel_id=1, replica_groups=mesh['zy'=8,'core'=2,'col'=8] {'col'}, dimensions={0} | all-to-all | bytes 2097152 | tf_op jit(solution)/shard_map/all_to_all | solution.py:208
  55.5 0.0 copy-done
  55.5 0.0 copy-done.1
  55.5 1.5 %shard_map.96 = (f32[1024,256]{1,0:T(8,128)S(1)}, bf16[8,640,128]{2,1,0:T(8,128)(2,1)S(1)}) custom-call(bf16[8,512,128]{2,1,0:T(8,128)(2,1)S(1)} %all_to_all.21.parts, bf16[64,256]{1,0:T(8,128)(2,1)S(1)} %copy-done.1, bf16[1024,256]{1,0:T(8,128)(2,1)S(1)} %copy-done), custom_call_target="tpu_custom_call" | custom-call | tf_op jit(solution)/shard_map/pallas_call | solution.py:161
  57.0 20.3 %all_to_all.22.grads = bf16[8,640,128]{2,1,0:T(8,128)(2,1)S(1)} all-to-all(bf16[8,640,128]{2,1,0:T(8,128)(2,1)S(1)} %get-tuple-element.14), channel_id=1, replica_groups=mesh['zy'=8,'core'=2,'col'=8] {'col'}, dimensions={0} | all-to-all | bytes 2621440 | tf_op jit(solution)/shard_map/all_to_all | solution.py:216
  77.3 2.8 %shard_map.97 = (f32[129,64,128]{2,1,0:T(8,128)S(1)}, bf16[4224,128]{1,0:T(8,128)(2,1)S(1)}) custom-call(s32[1,1]{1,0:T(1,128)S(6)} %copy.10.count, s32[1,1,384]{2,1,0:T(1,128)S(1)} %copy-done.2, s32[1,1,384]{2,1,0:T(1,128)S(1)} %copy-done.3, bf16[384,128,128]{2,1,0:T(8,128)(2,1)S(1)} %bitcast.6, bf16[8,640,128]{2,1,0:T(8,128)(2,1)S(1)} %all_to_all.22.grads), custom_call_target="tpu_custom_call" | custom-call | tf_op jit(solution)/shard_map/pallas_call | solution.py:161
  80.1 0.2 collective-permute-start.1
  80.3 1.1 shard_map.98
  81.4 1.5 %collective-permute-done.1.got = bf16[4224,128]{1,0:T(8,128)(2,1)S(1)} collective-permute-done((bf16[4224,128]{1,0:T(8,128)(2,1)S(1)}, bf16[4224,128]{1,0:T(8,128)(2,1)S(1)}, u32[]{:S(2)}, u32[]{:S(2)}) %collective-permute-start.1) | collective-permute-done | bytes 1081376 | tf_op jit(solution)/shard_map/ppermute | solution.py:229
  82.9 0.2 shard_map.99
  83.1 25.0 %all_to_all.23.parts = bf16[8,640,128]{2,1,0:T(8,128)(2,1)S(1)} all-to-all(bf16[8,640,128]{2,1,0:T(8,128)(2,1)S(1)} %shard_map.99), channel_id=1, replica_groups=mesh['zy'=8,'core'=2,'col'=8] {'zy'}, dimensions={0} | all-to-all | bytes 2621440 | tf_op jit(solution)/shard_map/all_to_all | solution.py:235
  108.1 0.8 shard_map.100
  (1 shorter events, 0.0 us)
Async XLA Ops:
  0.6 29.1 %slice-start = ((s8[12582912]{0:T(1024)(128)(4,1)}), s8[4194304]{0:T(1024)(128)(4,1)S(1)}, s32[]{:S(2)}) async-start(s8[12582912]{0:T(1024)(128)(4,1)} %bitcast.3), calls=%async_computation.4 | async-start | bytes 8388608
  0.6 1.1 copy-start.4
  1.7 28.1 %slice-start.1 = ((s8[12582912]{0:T(1024)(128)(4,1)}), s8[4194304]{0:T(1024)(128)(4,1)S(1)}, s32[]{:S(2)}) async-start(s8[12582912]{0:T(1024)(128)(4,1)} %bitcast.3), calls=%async_computation.5 | async-start | bytes 8388608
  1.7 28.1 %slice-start.2 = ((s8[12582912]{0:T(1024)(128)(4,1)}), s8[4194304]{0:T(1024)(128)(4,1)S(1)}, s32[]{:S(2)}) async-start(s8[12582912]{0:T(1024)(128)(4,1)} %bitcast.3), calls=%async_computation.6 | async-start | bytes 8388608
  1.8 28.0 %copy-start.2 = (s32[1,1,384]{2,1,0:T(1,128)S(1)}, s32[1,1,384]{2,1,0:T(1,128)}, u32[]{:S(2)}) copy-start(s32[1,1,384]{2,1,0:T(1,128)} %rows.3) | copy-start | bytes 4612
  1.8 28.0 %copy-start.3 = (s32[1,1,384]{2,1,0:T(1,128)S(1)}, s32[1,1,384]{2,1,0:T(1,128)}, u32[]{:S(2)}) copy-start(s32[1,1,384]{2,1,0:T(1,128)} %cols.3) | copy-start | bytes 4612
  27.1 2.7 %collective-permute-start = (bf16[8,64,1024]{2,1,0:T(8,128)(2,1)S(1)}, bf16[8,64,1024]{2,1,0:T(8,128)(2,1)S(1)}, u32[]{:S(2)}, u32[]{:S(2)}) collective-permute-start(bf16[8,64,1024]{2,1,0:T(8,128)(2,1)S(1)} %all_to_all.20.own), channel_id=1, source_target_pairs={{0,8},{8,0},{1,9},{9,1},{2,10},{10,2},{3,11},{11,3},{4,12},{12,4},... | collective-permute-start | bytes 3145736 | tf_op jit(solution)/shard_map/ppermute | solution.py:192
  33.3 22.2 %copy-start = (bf16[1024,256]{1,0:T(8,128)(2,1)S(1)}, bf16[1024,256]{1,0:T(8,128)(2,1)}, u32[]{:S(2)}) copy-start(bf16[1024,256]{1,0:T(8,128)(2,1)} %cotangent.1) | copy-start | bytes 1572868
  33.3 22.2 %copy-start.1 = (bf16[64,256]{1,0:T(8,128)(2,1)S(1)}, bf16[64,256]{1,0:T(8,128)(2,1)}, u32[]{:S(2)}) copy-start(bf16[64,256]{1,0:T(8,128)(2,1)} %weight.1) | copy-start | bytes 98308
  80.1 2.8 %collective-permute-start.1 = (bf16[4224,128]{1,0:T(8,128)(2,1)S(1)}, bf16[4224,128]{1,0:T(8,128)(2,1)S(1)}, u32[]{:S(2)}, u32[]{:S(2)}) collective-permute-start(bf16[4224,128]{1,0:T(8,128)(2,1)S(1)} %get-tuple-element.16.give), channel_id=1, source_target_pairs={{0,8},{8,0},{1,9},{9,1},{2,10},{10,2},{3,11},{11,3},{4,12},{12,4},... | collective-permute-start | bytes 3244040 | tf_op jit(solution)/shard_map/ppermute | solution.py:229

commit v6 on v5

--- a/solution.py
+++ b/solution.py
@@ -8,7 +8,7 @@
 from jax.sharding import Mesh, PartitionSpec as P
 
 SIDE = 128
-GROUP = 192
+FORWARD, BACKWARD = 384, 192
 LAG = 8
 MIB = 1024 * 1024
 f32 = jnp.float32
@@ -23,22 +23,22 @@
         out[chip] = features[...]
 
 
-def run_tiles(live, targets, values, total, product):
+def run_tiles(live, targets, values, total, product, size):
     dump = total.shape[0] - 1
     total[...] = jnp.zeros_like(total)
 
     def step(group, carry):
         products = []
-        for i in range(GROUP + LAG):
-            if i < GROUP:
-                products.append(product(group * GROUP + i))
+        for i in range(size + LAG):
+            if i < size:
+                products.append(product(group * size + i))
             if i >= LAG:
-                slot = group * GROUP + i - LAG
+                slot = group * size + i - LAG
                 target = jnp.where(slot < live, targets[0, 0, slot], dump)
                 total[target] += products[i - LAG]
         return carry
 
-    lax.fori_loop(0, (live + GROUP - 1) // GROUP, step, 0)
+    lax.fori_loop(0, (live + size - 1) // size, step, 0)
 
 
 def forward_kernel(count, rows, cols, values, own, other, out, total, source):
@@ -55,7 +55,7 @@
             values[slot], source[cols[0, 0, slot]], (((1,), (1,)), ((), ())), preferred_element_type=f32
         )
 
-    run_tiles(count[0, 0], rows, values, total, product)
+    run_tiles(count[0, 0], rows, values, total, product, FORWARD)
     per = out.shape[1] // SIDE
     for pair in range(out.shape[0] * per):
         at = (pair % per) * SIDE
@@ -112,7 +112,7 @@
         at = pl.multiple_of((pick & 7) * features, features)
         return jnp.dot(grads[pick >> 3, pl.ds(at, features), :], values[slot], preferred_element_type=f32)
 
-    run_tiles(count[0, 0], cols, values, total, product)
+    run_tiles(count[0, 0], cols, values, total, product, BACKWARD)
     chips = total.shape[0] // 16
     for chip in range(chips):
         for k in range(8):

time: 109 us -> 109 us (level)
  Pallas kernels: 9.95 us -> 11.8 us
  blocking collectives: 92.8 us -> 91.3 us
    pallas_call x7, Pallas kernels: 9.95 us -> 11.8 us  [call(): pl.pallas_call(kernel, out_shape=out_shape, in_specs=[SMEM_SPEC] * len(sc...]
    all_to_all x1, blocking collectives: 22.2 us -> 20.4 us  [on_device(): parts = lax.all_to_all(partial, 'col', 0, 0, tiled=True)]
where the time goes in v6:
time: 109 us
  blocking collectives  91.3 us (84%)
  Pallas kernels  11.8 us (11%)
  waiting for transfers between devices  3.6 us (3%)
  between operations  1.39 us (1%)
    all_to_all x1, blocking collectives, on_device(): own = lax.all_to_all(send, 'zy', 0, 0, tiled=True)  25.3 us
    all_to_all x1, blocking collectives, on_device(): parts = lax.all_to_all(send, 'zy', 0, 0, tiled=True)  25.2 us
    all_to_all x1, blocking collectives, on_device(): parts = lax.all_to_all(partial, 'col', 0, 0, tiled=True)  20.4 us
    all_to_all x1, blocking collectives, on_device(): grads = lax.all_to_all(send, 'col', 0, 0, tiled=True)  20.3 us
    pallas_call x7, Pallas kernels, call(): pl.pallas_call(kernel, out_shape=out_shape, in_specs=[SMEM_SPEC] * len(sc...  11.8 us
  transfers between devices with their start and end apart: 2, of which 2 were waited for; matrix products, arithmetic and copies ran while one was open for 0% of the time, Pallas kernels for 1%

profile of v6, /device:TPU:0, one launch (start us, length us, event | category | flops | bytes accessed | tf_op | source)
XLA Modules:
  0.0 109.3 jit_solution(14021400727044047490)
XLA Ops:
  0.6 0.0 slice-start
  0.6 0.0 copy-start.4
  0.7 1.0 copy-done.4
  1.7 0.0 slice-start.1
  1.7 0.0 slice-start.2
  1.7 0.1 shard_map.94
  1.8 0.0 copy-start.2
  1.8 0.0 copy-start.3
  1.8 25.3 %all_to_all.20.own = bf16[8,64,1024]{2,1,0:T(8,128)(2,1)S(1)} all-to-all(bf16[8,64,1024]{2,1,0:T(8,128)(2,1)S(1)} %shard_map.94), channel_id=1, replica_groups=mesh['zy'=8,'core'=2,'col'=8] {'zy'}, dimensions={0} | all-to-all | bytes 2097152 | tf_op jit(solution)/shard_map/all_to_all | solution.py:191
  27.1 0.0 collective-permute-start
  27.7 2.0 %collective-permute-done.other = bf16[8,64,1024]{2,1,0:T(8,128)(2,1)S(1)} collective-permute-done((bf16[8,64,1024]{2,1,0:T(8,128)(2,1)S(1)}, bf16[8,64,1024]{2,1,0:T(8,128)(2,1)S(1)}, u32[]{:S(2)}, u32[]{:S(2)}) %collective-permute-start) | collective-permute-done | bytes 1048608 | tf_op jit(solution)/shard_map/ppermute | solution.py:192
  29.7 0.0 slice-done
  29.8 0.0 slice-done.1
  29.8 0.0 slice-done.2
  29.8 0.0 copy-done.2
  29.8 0.0 copy-done.3
  29.8 5.3 %shard_map.95 = bf16[8,512,128]{2,1,0:T(8,128)(2,1)S(1)} custom-call(s32[1,1]{1,0:T(1,128)S(6)} %copy.10.count, s32[1,1,384]{2,1,0:T(1,128)S(1)} %copy-done.2, s32[1,1,384]{2,1,0:T(1,128)S(1)} %copy-done.3, bf16[384,128,128]{2,1,0:T(8,128)(2,1)S(1)} %bitcast.5, bf16[8,64,1024]{2,1,0:T(8,128)(2,1)S(1)} %all_to_all.20.own, ...), custom_call_target="tpu_custom_call" | custom-call | tf_op jit(solution)/shard_map/pallas_call | solution.py:161
  35.1 0.0 copy-start
  35.1 0.0 copy-start.1
  35.1 20.4 %all_to_all.21.parts = bf16[8,512,128]{2,1,0:T(8,128)(2,1)S(1)} all-to-all(bf16[8,512,128]{2,1,0:T(8,128)(2,1)S(1)} %shard_map.95), channel_id=1, replica_groups=mesh['zy'=8,'core'=2,'col'=8] {'col'}, dimensions={0} | all-to-all | bytes 2097152 | tf_op jit(solution)/shard_map/all_to_all | solution.py:208
  55.6 0.0 copy-done
  55.6 0.0 copy-done.1
  55.6 1.5 %shard_map.96 = (f32[1024,256]{1,0:T(8,128)S(1)}, bf16[8,640,128]{2,1,0:T(8,128)(2,1)S(1)}) custom-call(bf16[8,512,128]{2,1,0:T(8,128)(2,1)S(1)} %all_to_all.21.parts, bf16[64,256]{1,0:T(8,128)(2,1)S(1)} %copy-done.1, bf16[1024,256]{1,0:T(8,128)(2,1)S(1)} %copy-done), custom_call_target="tpu_custom_call" | custom-call | tf_op jit(solution)/shard_map/pallas_call | solution.py:161
  57.1 20.3 %all_to_all.22.grads = bf16[8,640,128]{2,1,0:T(8,128)(2,1)S(1)} all-to-all(bf16[8,640,128]{2,1,0:T(8,128)(2,1)S(1)} %get-tuple-element.14), channel_id=1, replica_groups=mesh['zy'=8,'core'=2,'col'=8] {'col'}, dimensions={0} | all-to-all | bytes 2621440 | tf_op jit(solution)/shard_map/all_to_all | solution.py:216
  77.4 2.8 %shard_map.97 = (f32[129,64,128]{2,1,0:T(8,128)S(1)}, bf16[4224,128]{1,0:T(8,128)(2,1)S(1)}) custom-call(s32[1,1]{1,0:T(1,128)S(6)} %copy.10.count, s32[1,1,384]{2,1,0:T(1,128)S(1)} %copy-done.2, s32[1,1,384]{2,1,0:T(1,128)S(1)} %copy-done.3, bf16[384,128,128]{2,1,0:T(8,128)(2,1)S(1)} %bitcast.6, bf16[8,640,128]{2,1,0:T(8,128)(2,1)S(1)} %all_to_all.22.grads), custom_call_target="tpu_custom_call" | custom-call | tf_op jit(solution)/shard_map/pallas_call | solution.py:161
  80.2 0.1 collective-permute-start.1
  80.3 1.1 shard_map.98
  81.4 1.6 %collective-permute-done.1.got = bf16[4224,128]{1,0:T(8,128)(2,1)S(1)} collective-permute-done((bf16[4224,128]{1,0:T(8,128)(2,1)S(1)}, bf16[4224,128]{1,0:T(8,128)(2,1)S(1)}, u32[]{:S(2)}, u32[]{:S(2)}) %collective-permute-start.1) | collective-permute-done | bytes 1081376 | tf_op jit(solution)/shard_map/ppermute | solution.py:229
  83.0 0.2 shard_map.99
  83.2 25.2 %all_to_all.23.parts = bf16[8,640,128]{2,1,0:T(8,128)(2,1)S(1)} all-to-all(bf16[8,640,128]{2,1,0:T(8,128)(2,1)S(1)} %shard_map.99), channel_id=1, replica_groups=mesh['zy'=8,'core'=2,'col'=8] {'zy'}, dimensions={0} | all-to-all | bytes 2621440 | tf_op jit(solution)/shard_map/all_to_all | solution.py:235
  108.4 0.8 shard_map.100
  (1 shorter events, 0.0 us)
Async XLA Ops:
  0.6 29.1 %slice-start = ((s8[12582912]{0:T(1024)(128)(4,1)}), s8[4194304]{0:T(1024)(128)(4,1)S(1)}, s32[]{:S(2)}) async-start(s8[12582912]{0:T(1024)(128)(4,1)} %bitcast.3), calls=%async_computation.4 | async-start | bytes 8388608
  0.6 1.1 copy-start.4
  1.7 28.1 %slice-start.1 = ((s8[12582912]{0:T(1024)(128)(4,1)}), s8[4194304]{0:T(1024)(128)(4,1)S(1)}, s32[]{:S(2)}) async-start(s8[12582912]{0:T(1024)(128)(4,1)} %bitcast.3), calls=%async_computation.5 | async-start | bytes 8388608
  1.7 28.1 %slice-start.2 = ((s8[12582912]{0:T(1024)(128)(4,1)}), s8[4194304]{0:T(1024)(128)(4,1)S(1)}, s32[]{:S(2)}) async-start(s8[12582912]{0:T(1024)(128)(4,1)} %bitcast.3), calls=%async_computation.6 | async-start | bytes 8388608
  1.8 28.0 %copy-start.2 = (s32[1,1,384]{2,1,0:T(1,128)S(1)}, s32[1,1,384]{2,1,0:T(1,128)}, u32[]{:S(2)}) copy-start(s32[1,1,384]{2,1,0:T(1,128)} %rows.3) | copy-start | bytes 4612
  1.8 28.0 %copy-start.3 = (s32[1,1,384]{2,1,0:T(1,128)S(1)}, s32[1,1,384]{2,1,0:T(1,128)}, u32[]{:S(2)}) copy-start(s32[1,1,384]{2,1,0:T(1,128)} %cols.3) | copy-start | bytes 4612
  27.1 2.7 %collective-permute-start = (bf16[8,64,1024]{2,1,0:T(8,128)(2,1)S(1)}, bf16[8,64,1024]{2,1,0:T(8,128)(2,1)S(1)}, u32[]{:S(2)}, u32[]{:S(2)}) collective-permute-start(bf16[8,64,1024]{2,1,0:T(8,128)(2,1)S(1)} %all_to_all.20.own), channel_id=1, source_target_pairs={{0,8},{8,0},{1,9},{9,1},{2,10},{10,2},{3,11},{11,3},{4,12},{12,4},... | collective-permute-start | bytes 3145736 | tf_op jit(solution)/shard_map/ppermute | solution.py:192
  35.1 20.5 %copy-start = (bf16[1024,256]{1,0:T(8,128)(2,1)S(1)}, bf16[1024,256]{1,0:T(8,128)(2,1)}, u32[]{:S(2)}) copy-start(bf16[1024,256]{1,0:T(8,128)(2,1)} %cotangent.1) | copy-start | bytes 1572868
  35.1 20.4 %copy-start.1 = (bf16[64,256]{1,0:T(8,128)(2,1)S(1)}, bf16[64,256]{1,0:T(8,128)(2,1)}, u32[]{:S(2)}) copy-start(bf16[64,256]{1,0:T(8,128)(2,1)} %weight.1) | copy-start | bytes 98308
  80.2 2.8 %collective-permute-start.1 = (bf16[4224,128]{1,0:T(8,128)(2,1)S(1)}, bf16[4224,128]{1,0:T(8,128)(2,1)S(1)}, u32[]{:S(2)}, u32[]{:S(2)}) collective-permute-start(bf16[4224,128]{1,0:T(8,128)(2,1)S(1)} %get-tuple-element.16.give), channel_id=1, source_target_pairs={{0,8},{8,0},{1,9},{9,1},{2,10},{10,2},{3,11},{11,3},{4,12},{12,4},... | collective-permute-start | bytes 3244040 | tf_op jit(solution)/shard_map/ppermute | solution.py:229
